TPU v7x, 32 devices: a whole 2x2x4 slice. The times are simulated.
32 devices in a mesh: dp: 8 (over y, x, core), tensor: 4 (over z).
Axes of the slice: x: 2, y: 2, z: 4, core: 2. Of those that a mesh axis runs over, the one named last changes fastest.
Arguments:
- tokens: bfloat16 [4096, 768], P(('dp', 'tensor')), may hold values from -6 to 6
- doc_ids: int32 [4096], P('dp'), may hold values from 0 to 2, as said below
- expert_ids: int32 [4096, 1], P('dp'), may hold values from 0 to 3; in each aligned block of 512 rows (0 to 511, 512 to 1023, ...) at most 144 rows name the same one
- cotangent: bfloat16 [4096, 768], P(('dp', 'tensor')), may hold values from -6 to 6
- w_query: bfloat16 [768, 768], P('dp', 'tensor'), may hold values from -0.0546875 to 0.0546875
- w_key: bfloat16 [768, 768], P('dp', 'tensor'), may hold values from -0.21875 to 0.21875
- w_value: bfloat16 [768, 768], P('dp', 'tensor'), may hold values from -0.21875 to 0.21875
- w_attn_out: bfloat16 [768, 768], P('tensor', 'dp'), may hold values from -1.25 to 1.25
- gain_attn: float32 [768], replicated, may hold values from 0.5 to 1.5
- gain_expert: float32 [768], replicated, may hold values from 0.5 to 1.5
- rel_bias: float32 [32, 12], replicated, may hold values from -3 to 3
- w_router: bfloat16 [768, 4], P('dp'), may hold values from -0.15625 to 0.15625
- w_expert_in: bfloat16 [4, 768, 3072], P(None, 'dp', 'tensor'), may hold values from -0.21875 to 0.21875
- w_expert_out: bfloat16 [4, 3072, 768], P(None, 'tensor', 'dp'), may hold values from -0.4375 to 0.4375
Outputs:
- layer_out: bfloat16 [4096, 768], P(('dp', 'tensor'))
- grad_tokens: bfloat16 [4096, 768], P(('dp', 'tensor'))
- grad_query: float32 [768, 768], P('dp', 'tensor')
- grad_key: float32 [768, 768], P('dp', 'tensor')
- grad_value: float32 [768, 768], P('dp', 'tensor')
- grad_attn_out: float32 [768, 768], P('tensor', 'dp')
- grad_gain_attn: float32 [768], replicated
- grad_gain_expert: float32 [768], replicated
- grad_rel_bias: float32 [32, 12], replicated
- grad_router: float32 [768, 4], P('dp')
- grad_expert_in: float32 [4, 768, 3072], P(None, 'dp', 'tensor')
- grad_expert_out: float32 [4, 3072, 768], P(None, 'tensor', 'dp')
Inputs may be any that keep to these rules, and one draw needn't show every extreme that they name: `doc_ids`: within each group of 512 rows the numbers never fall; every group has a document 1 that begins in the group's first fifth and ends in its last fifth, and some group holds document 1 alone over all its rows. `expert_ids`: among the 512 rows of one group at most 144 name the same expert.
All inputs are finite; a program needn't handle non-finite values.
Results may differ from a plain program's by a relative error of at most 0.014.
The roundings to bfloat16 on the way count: a program that leaves them out, or rounds other values in their place, can miss the bound.
Values may be sent and summed in bfloat16 or wider, within the bound.
A program may use at most 192 MiB of HBM per device.

v0:
```python
import functools

import jax
import jax.numpy as jnp
import numpy as np
from jax import lax
from jax.experimental import pallas as pl
from jax.experimental.pallas import tpu as pltpu
from jax.sharding import PartitionSpec as P

HEAD_DIM = 64
BUCKETS = 32
MAX_DIST = 128


norm_eps = 1e-06
masked_score = -1e30


def bucket_table(length, buckets, max_reach):
    half_count = buckets // 2
    exact_count = half_count // 2
    positions = np.arange(length)
    offset = positions[None, :] - positions[:, None]
    distance = np.abs(offset)
    far_bucket = exact_count + (
        np.log(np.maximum(distance, 1) / exact_count)
        / np.log(max_reach / exact_count)
        * (half_count - exact_count)
    ).astype(np.int64)
    far_bucket = np.minimum(far_bucket, half_count - 1)
    bucket = np.where(distance < exact_count, distance, far_bucket) + half_count * (offset > 0)
    return bucket.astype(np.int32)


def rms_scale(values):
    return lax.rsqrt(jnp.mean(values * values, axis=-1, keepdims=True) + norm_eps)


def gelu_tanh(values):
    return jax.nn.gelu(values, approximate=True)


pieces = 4
vmem_bytes = 48 * 1024 * 1024


def greet_line(barrier, axis, size):
    me = lax.axis_index(axis)
    for side, there in ((1, me < size - 1), (-1, me > 0)):

        @pl.when(there)
        def greet(side=side):
            pl.semaphore_signal(
                barrier,
                inc=1,
                device_id={axis: me + side},
                device_id_type=pl.DeviceIdType.MESH,
            )

    return (me < size - 1).astype(jnp.int32) + (me > 0).astype(jnp.int32)


def line_gather(axis, size, x_ref, out_ref, send_sem, recv_sem):
    me = lax.axis_index(axis)
    rows = x_ref.shape[0] // pieces

    def hop(way, step, piece):
        side = 1 - 2 * way
        block = me - side * step
        part = pl.ds(piece * rows, rows)
        return pltpu.make_async_remote_copy(
            src_ref=x_ref.at[part] if step == 0 else out_ref.at[block, part],
            dst_ref=out_ref.at[block, part],
            send_sem=send_sem.at[way, step, piece],
            recv_sem=recv_sem.at[way, step, piece],
            device_id={axis: me + side},
            device_id_type=pl.DeviceIdType.MESH,
        )

    def arrival(way, step, piece):
        side = 1 - 2 * way
        block = me - side * (step + 1)
        part = pl.ds(piece * rows, rows)
        return pltpu.make_async_remote_copy(
            src_ref=x_ref.at[part],
            dst_ref=out_ref.at[block, part],
            send_sem=send_sem.at[way, step, piece],
            recv_sem=recv_sem.at[way, step, piece],
            device_id={axis: me + side},
            device_id_type=pl.DeviceIdType.MESH,
        )

    def sends(way, step):
        if way == 0:
            return (me < size - 1) & (me >= step)
        return (me > 0) & (me + step <= size - 1)

    def receives(way, step):
        if way == 0:
            return me >= step + 1
        return me + step + 1 <= size - 1

    for step in range(size):
        for piece in range(pieces):
            for way in range(2):
                if step > 0:

                    @pl.when(receives(way, step - 1))
                    def landed(way=way, step=step, piece=piece):
                        arrival(way, step - 1, piece).wait_recv()

                if step < size - 1:

                    @pl.when(sends(way, step))
                    def forward(way=way, step=step, piece=piece):
                        hop(way, step, piece).start()

    for step in range(size - 1):
        for piece in range(pieces):
            for way in range(2):

                @pl.when(sends(way, step))
                def gone(way=way, step=step, piece=piece):
                    hop(way, step, piece).wait_send()


def line_sum_kernel(axis, size, x_ref, out_ref, got, going, send_sem, recv_sem):
    me = lax.axis_index(axis)
    barrier = pltpu.get_barrier_semaphore()
    pl.semaphore_wait(barrier, greet_line(barrier, axis, size))
    rows = x_ref.shape[1] // pieces

    def hop(way, dest, piece):
        part = pl.ds(piece * rows, rows)
        return pltpu.make_async_remote_copy(
            src_ref=going.at[way, dest, part],
            dst_ref=got.at[way, dest, part],
            send_sem=send_sem.at[way, dest, piece],
            recv_sem=recv_sem.at[way, dest, piece],
            device_id={axis: me + 1 - 2 * way},
            device_id_type=pl.DeviceIdType.MESH,
        )

    def before(way, dest):
        return me < dest if way == 0 else me > dest

    def first(way):
        return me == 0 if way == 0 else me == size - 1

    for order in range(size - 1):
        for piece in range(pieces):
            for way in range(2):
                dest = size - 1 - order if way == 0 else order
                part = pl.ds(piece * rows, rows)

                @pl.when(before(way, dest) & first(way))
                def begin(way=way, dest=dest, part=part):
                    going[way, dest, part] = x_ref[dest, part]

                @pl.when(before(way, dest) & jnp.logical_not(first(way)))
                def add(way=way, dest=dest, part=part, piece=piece):
                    hop(way, dest, piece).wait_recv()
                    going[way, dest, part] = (
                        x_ref[dest, part].astype(jnp.float32)
                        + got[way, dest, part].astype(jnp.float32)
                    ).astype(jnp.bfloat16)

                @pl.when(before(way, dest))
                def send(way=way, dest=dest, piece=piece):
                    hop(way, dest, piece).start()

    out_ref[...] = x_ref[me].astype(jnp.float32)
    for way in range(2):

        @pl.when(jnp.logical_not(first(way)))
        def finish(way=way):
            for piece in range(pieces):
                hop(way, me, piece).wait_recv()
            out_ref[...] += got[way, me].astype(jnp.float32)

    for dest in range(size):
        for piece in range(pieces):
            for way in range(2):

                @pl.when(before(way, dest))
                def gone(way=way, dest=dest, piece=piece):
                    hop(way, dest, piece).wait_send()


def line_sum(ident, x, axis):
    size = lax.axis_size(axis)
    block = pl.BlockSpec(memory_space=pltpu.VMEM)
    return pl.pallas_call(
        functools.partial(line_sum_kernel, axis, size),
        out_shape=jax.ShapeDtypeStruct(x.shape[1:], jnp.float32),
        in_specs=[block],
        out_specs=block,
        scratch_shapes=[
            pltpu.VMEM((2,) + x.shape, x.dtype),
            pltpu.VMEM((2,) + x.shape, x.dtype),
            pltpu.SemaphoreType.DMA((2, size, pieces)),
            pltpu.SemaphoreType.DMA((2, size, pieces)),
        ],
        compiler_params=pltpu.CompilerParams(
            collective_id=ident, has_side_effects=True, vmem_limit_bytes=vmem_bytes
        ),
    )(x)


def attend_kernel(head_width, normed_ref, weights_ref, base_ref, doc_col, doc_row, proj_ref, prob_ref, mixed_ref, sent_ref, bias):
    rows = normed_ref.shape[0]
    proj_ref[...] = dot_nn(normed_ref[...], weights_ref[:, : 3 * head_width]).astype(jnp.bfloat16)
    same = doc_col[...] == doc_row[...]
    mixed = []
    for head in range(head_width // HEAD_DIM):
        query, key, value = (
            proj_ref[:, part * head_width + head * HEAD_DIM : part * head_width + (head + 1) * HEAD_DIM]
            for part in range(3)
        )
        base = base_ref[head]
        for block in range(rows // 8):
            turned = base if block == 0 else pltpu.roll(base, 8 * block, 1)
            bias[8 * block : 8 * block + 8, :] = turned[:, :rows]
        scores = jnp.where(same, dot_nt(query, key) + bias[...], masked_score)
        exps = jnp.exp(scores - jnp.max(scores, axis=-1, keepdims=True))
        probs = exps / jnp.sum(exps, axis=-1, keepdims=True)
        prob_ref[head] = probs
        mixed.append(dot_nn(probs.astype(jnp.bfloat16), value).astype(jnp.bfloat16))
    mixed_ref[...] = jnp.concatenate(mixed, axis=1)
    sent_ref[...] = dot_nt(
        mixed_ref[...], weights_ref[:, 3 * head_width : 4 * head_width]
    ).astype(jnp.bfloat16)


def attend_back_kernel(head_width, grad_ref, weights_ref, proj_ref, prob_ref, grads_ref, sent_ref, diag_ref, wide):
    rows = grad_ref.shape[0]
    grad_mixed = dot_nn(
        grad_ref[...], weights_ref[:, 3 * head_width : 4 * head_width]
    ).astype(jnp.bfloat16)
    grads = [[], [], []]
    wide[:, rows:] = jnp.zeros((rows, rows), jnp.float32)
    for head in range(head_width // HEAD_DIM):
        query, key, value = (
            proj_ref[:, part * head_width + head * HEAD_DIM : part * head_width + (head + 1) * HEAD_DIM]
            for part in range(3)
        )
        grad_head = grad_mixed[:, head * HEAD_DIM : (head + 1) * HEAD_DIM]
        probs = prob_ref[head]
        grad_probs = dot_nt(grad_head, value)
        row_dot = jnp.sum(probs * grad_probs, axis=-1, keepdims=True)
        grad_scores = (probs * (grad_probs - row_dot)).astype(jnp.bfloat16)
        grads[0].append(dot_nn(grad_scores, key).astype(jnp.bfloat16))
        grads[1].append(dot_tn(grad_scores, query).astype(jnp.bfloat16))
        grads[2].append(dot_tn(probs.astype(jnp.bfloat16), grad_head).astype(jnp.bfloat16))
        wide[:, :rows] = grad_scores.astype(jnp.float32)
        total = wide[0:8, :]
        for block in range(1, rows // 8):
            total = total + pltpu.roll(wide[8 * block : 8 * block + 8, :], 2 * rows - 8 * block, 1)
        diag_ref[head] = total
    grads_ref[...] = jnp.concatenate(grads[0] + grads[1] + grads[2], axis=1)
    sent_ref[...] = dot_nt(grads_ref[...], weights_ref[:, : 3 * head_width]).astype(jnp.bfloat16)


def bucket_onehot(length):
    spread = np.arange(2 * length)[None, :] - np.arange(8)[:, None]
    spread = (spread + length) % (2 * length) - length
    table = bucket_table(length, BUCKETS, MAX_DIST)
    line = np.concatenate([table[:, 0][::-1], table[0, 1:]])
    picked = line[np.clip(spread + length - 1, 0, 2 * length - 2)]
    return (picked[None] == np.arange(BUCKETS)[:, None, None]).astype(np.float32)


def exchange_kernel(plan, sizes, *refs):
    count = len(plan)
    ins, outs = refs[:count], refs[count : 2 * count]
    send_sem, recv_sem, own_sem, line_send, line_recv = refs[2 * count :]
    barrier = pltpu.get_barrier_semaphore()
    greeted = 0
    direct = {axis for axis, kind in plan if kind != "line"}
    for axis, size in sizes:
        me = lax.axis_index(axis)
        if axis not in direct:
            greeted += greet_line(barrier, axis, size)
            continue
        for step in range(1, size):
            pl.semaphore_signal(
                barrier,
                inc=1,
                device_id={axis: lax.rem(me + step, size)},
                device_id_type=pl.DeviceIdType.MESH,
            )
        greeted += size - 1
    pl.semaphore_wait(barrier, greeted)
    size_of = dict(sizes)
    copies = []
    for step in range(1, max(size_of.values())):
        for num, (axis, kind) in enumerate(plan):
            size = size_of[axis]
            if step >= size or kind == "line":
                continue
            me = lax.axis_index(axis)
            peer = lax.rem(me + step, size)
            copy = pltpu.make_async_remote_copy(
                src_ref=ins[num] if kind == "gather" else ins[num].at[peer],
                dst_ref=outs[num].at[me],
                send_sem=send_sem.at[num, step],
                recv_sem=recv_sem.at[num, step],
                device_id={axis: peer},
                device_id_type=pl.DeviceIdType.MESH,
            )
            copy.start()
            copies.append(copy)
    for num, (axis, kind) in enumerate(plan):
        me = lax.axis_index(axis)
        own = pltpu.make_async_copy(
            ins[num].at[me] if kind == "swap" else ins[num], outs[num].at[me], own_sem.at[num]
        )
        own.start()
        copies.append(own)
    for num, (axis, kind) in enumerate(plan):
        if kind == "line":
            line_gather(
                axis, size_of[axis], ins[num], outs[num], line_send.at[num], line_recv.at[num]
            )
    for copy in copies:
        copy.wait()


def exchange(ident, items):
    plan = tuple((axis, kind) for unused, axis, kind in items)
    axes = sorted({axis for axis, unused in plan})
    sizes = tuple((axis, lax.axis_size(axis)) for axis in axes)
    size_of = dict(sizes)
    shapes = [
        jax.ShapeDtypeStruct(
            ((size_of[axis],) + x.shape) if kind != "swap" else x.shape, x.dtype
        )
        for x, axis, kind in items
    ]
    most = max(size_of.values())
    return pl.pallas_call(
        functools.partial(exchange_kernel, plan, sizes),
        out_shape=shapes,
        in_specs=[pl.BlockSpec(memory_space=pl.ANY)] * len(items),
        out_specs=[pl.BlockSpec(memory_space=pl.ANY)] * len(items),
        scratch_shapes=[
            pltpu.SemaphoreType.DMA((len(items), most)),
            pltpu.SemaphoreType.DMA((len(items), most)),
            pltpu.SemaphoreType.DMA((len(items),)),
            pltpu.SemaphoreType.DMA((len(items), 2, most, pieces)),
            pltpu.SemaphoreType.DMA((len(items), 2, most, pieces)),
        ],
        compiler_params=pltpu.CompilerParams(collective_id=ident, has_side_effects=True),
    )(*[x for x, unused, unused2 in items])


def dot_nn(left, right):
    return jnp.dot(left, right, preferred_element_type=jnp.float32)


def dot_nt(left, right):
    return lax.dot_general(left, right, (((1,), (1,)), ((), ())), preferred_element_type=jnp.float32)


def dot_tn(left, right):
    return lax.dot_general(left, right, (((0,), (0,)), ((), ())), preferred_element_type=jnp.float32)


def sum_parts(parts):
    return jnp.sum(parts.astype(jnp.float32), axis=0)


def norm_backward(grad_out, inputs_in, scale_in, gain_vec):
    scaled = grad_out * gain_vec
    grad_in = scale_in * scaled - inputs_in * scale_in**3 * jnp.mean(
        scaled * inputs_in, axis=-1, keepdims=True
    )
    grad_gain = jnp.sum(grad_out * inputs_in * scale_in, axis=0)
    return (grad_in, grad_gain)


def body(
    tokens,
    doc_ids,
    expert_ids,
    cotangent,
    w_query,
    w_key,
    w_value,
    w_attn_out,
    gain_attn,
    gain_expert,
    rel_bias,
    w_router,
    w_expert_in,
    w_expert_out,
):
    tensor_count = lax.axis_size("tensor")
    group_count = lax.axis_size("dp")
    local_rows = tokens.shape[0]
    group_rows = local_rows * tensor_count
    model_width = tokens.shape[1]
    width_share = model_width // group_count
    my_start = lax.axis_index("tensor") * local_rows
    expert_count = w_router.shape[1]
    serve_count = group_count // expert_count
    base_slots = 9 * group_rows // (8 * expert_count)
    capacity = (base_slots + serve_count - 1) // serve_count * serve_count
    slot_count = expert_count * capacity
    share_rows = capacity // serve_count
    share_pad = (share_rows + 15) // 16 * 16
    head_width = w_query.shape[1]
    head_count = head_width // HEAD_DIM
    bf = jnp.bfloat16
    sent_attn = jnp.concatenate(
        [
            w_query,
            w_key,
            w_value,
            w_attn_out.T,
            jnp.pad(w_router, ((0, 0), (0, 128 - expert_count))),
        ],
        axis=1,
    )
    sent_experts = jnp.repeat(
        jnp.stack([w_expert_in, w_expert_out.transpose(0, 2, 1)], axis=1), serve_count, axis=0
    )
    hidden_share = w_expert_in.shape[2]
    head_start = lax.axis_index("tensor") * head_count
    rel_local = lax.dynamic_slice_in_dim(rel_bias, head_start, head_count, 1)
    route_ids = expert_ids[:, 0]
    input_f = tokens.astype(jnp.float32)
    scale_one = rms_scale(input_f)
    sent_one = (input_f * scale_one * gain_attn).astype(bf)
    normed_parts, attn_parts = exchange(
        1, [(sent_one, "tensor", "line"), (sent_attn, "dp", "gather")]
    )
    expert_parts = lax.all_to_all(sent_experts, "dp", split_axis=0, concat_axis=0, tiled=True)
    normed_one = normed_parts.reshape(group_rows, model_width)
    attn_full = attn_parts.reshape(model_width, sent_attn.shape[1])
    router_full = attn_full[:, 4 * head_width : 4 * head_width + expert_count]
    onehot = jnp.asarray(bucket_onehot(group_rows))
    rel_base = jnp.einsum(
        "bh,brt->hrt", rel_local, onehot, precision=lax.Precision.HIGHEST
    )
    vmem_block = pl.BlockSpec(memory_space=pltpu.VMEM)
    projected, probs, mixed_all, attn_sent = pl.pallas_call(
        functools.partial(attend_kernel, head_width),
        out_shape=[
            jax.ShapeDtypeStruct((group_rows, 3 * head_width), bf),
            jax.ShapeDtypeStruct((head_count, group_rows, group_rows), jnp.float32),
            jax.ShapeDtypeStruct((group_rows, head_width), bf),
            jax.ShapeDtypeStruct((group_rows, model_width), bf),
        ],
        in_specs=[vmem_block] * 5,
        out_specs=[vmem_block] * 4,
        scratch_shapes=[pltpu.VMEM((group_rows, group_rows), jnp.float32)],
        compiler_params=pltpu.CompilerParams(vmem_limit_bytes=vmem_bytes),
    )(normed_one, attn_full, rel_base, doc_ids[:, None], doc_ids[None, :])
    attn_sum_local = line_sum(
        2, attn_sent.reshape(tensor_count, local_rows, model_width), "tensor"
    )
    middle = input_f + attn_sum_local
    scale_two = rms_scale(middle)
    normed_local = (middle * scale_two * gain_expert).astype(bf)
    normed_two, grad_full = exchange(
        3, [(normed_local, "tensor", "line"), (cotangent, "tensor", "line")]
    )
    normed_two = normed_two.reshape(group_rows, model_width)
    grad_full = grad_full.reshape(group_rows, model_width)
    logits = dot_nn(normed_two, router_full)
    gate_probs = jax.nn.softmax(logits, axis=-1)
    chosen = route_ids[:, None] == jnp.arange(expert_count)[None, :]
    gate_value = jnp.sum(jnp.where(chosen, gate_probs, 0.0), axis=-1)
    earlier = jnp.asarray(np.tril(np.ones((group_rows, group_rows), np.float32), -1), bf)
    counts = dot_nn(earlier, chosen.astype(bf))
    slot_index = jnp.sum(jnp.where(chosen, counts, 0.0), axis=-1).astype(jnp.int32)
    server = route_ids * serve_count + slot_index // share_rows
    slot_place = server * share_pad + slot_index % share_rows
    place = (
        slot_place[None, :] == jnp.arange(group_count * share_pad, dtype=jnp.int32)[:, None]
    ).astype(bf)
    grad_f = grad_full.astype(jnp.float32)
    gated = (gate_value[:, None] * grad_f).astype(bf)
    both = dot_nn(place, jnp.concatenate([normed_two, gated], axis=1)).astype(bf)
    (recv_both,) = exchange(
        4, [(both.reshape(group_count, share_pad, 2 * model_width), "dp", "swap")]
    )
    recv_both = recv_both.reshape(group_count * share_pad, 2 * model_width)
    rows_mine = recv_both[:, :model_width]
    grad_mine = recv_both[:, model_width:]
    inner_mine = expert_parts[:, 0].reshape(model_width, hidden_share)
    outer_mine = expert_parts[:, 1].reshape(model_width, hidden_share)
    inner_pre = dot_nn(rows_mine, inner_mine)
    inner_act, gelu_pull = jax.vjp(gelu_tanh, inner_pre)
    inner_act = inner_act.astype(bf)
    expert_part = dot_nt(inner_act, outer_mine).astype(bf)
    grad_pre = gelu_pull(dot_nn(grad_mine, outer_mine))[0].astype(bf)
    grad_rows = dot_nt(grad_pre, inner_mine).astype(bf)
    (back_both,) = exchange(
        5,
        [
            (
                jnp.concatenate([expert_part, grad_rows], axis=1).reshape(
                    group_count, share_pad, 2 * model_width
                ),
                "dp",
                "swap",
            )
        ],
    )
    inner_grad = dot_tn(rows_mine, grad_pre).astype(bf)
    outer_grad = dot_tn(grad_mine, inner_act).astype(bf)
    weight_back = lax.all_to_all(
        jnp.stack(
            [
                inner_grad.reshape(group_count, width_share, hidden_share),
                outer_grad.reshape(group_count, width_share, hidden_share),
            ],
            axis=1,
        ),
        "dp",
        split_axis=0,
        concat_axis=0,
        tiled=True,
    )
    weight_sum = jnp.sum(
        weight_back.reshape(
            expert_count, serve_count, 2, width_share, hidden_share
        ).astype(jnp.float32),
        axis=1,
    )
    inner_sum = weight_sum[:, 0]
    outer_sum = weight_sum[:, 1].transpose(0, 2, 1)
    returned = dot_tn(place, back_both.reshape(group_count * share_pad, 2 * model_width)).astype(bf)
    row_sum = line_sum(6, returned.reshape(tensor_count, local_rows, 2 * model_width), "tensor")
    expert_local = row_sum[:, :model_width]
    gate_local = lax.dynamic_slice_in_dim(gate_value, my_start, local_rows, 0)
    layer_out = (middle + gate_local[:, None] * expert_local).astype(bf)
    cot_local = cotangent.astype(jnp.float32)
    gate_grad = jnp.sum(cot_local * expert_local, axis=-1)
    probs_local = lax.dynamic_slice_in_dim(gate_probs, my_start, local_rows, 0)
    chosen_local = lax.dynamic_slice_in_dim(chosen.astype(jnp.float32), my_start, local_rows, 0)
    grad_logits = (probs_local * gate_grad[:, None] * (chosen_local - gate_local[:, None])).astype(
        jnp.bfloat16
    )
    grad_router_part = jnp.einsum(
        "qd,qe->de", normed_local, grad_logits, preferred_element_type=jnp.float32
    )
    router_term = jnp.einsum(
        "qe,de->qd", grad_logits, router_full, preferred_element_type=jnp.float32
    )
    grad_two_local = row_sum[:, model_width:] + router_term
    grad_mid, grad_gain_two = norm_backward(grad_two_local, middle, scale_two, gain_expert)
    grad_middle = cot_local + grad_mid
    (grad_mid_full,) = exchange(7, [(grad_middle.astype(bf), "tensor", "line")])
    grad_mid_full = grad_mid_full.reshape(group_rows, model_width)
    grad_out_w = dot_tn(grad_mid_full, mixed_all)
    grad_qkv, grad_one_sent, diagonals = pl.pallas_call(
        functools.partial(attend_back_kernel, head_width),
        out_shape=[
            jax.ShapeDtypeStruct((group_rows, 3 * head_width), bf),
            jax.ShapeDtypeStruct((group_rows, model_width), bf),
            jax.ShapeDtypeStruct((head_count, 8, 2 * group_rows), jnp.float32),
        ],
        in_specs=[vmem_block] * 4,
        out_specs=[vmem_block] * 3,
        scratch_shapes=[pltpu.VMEM((group_rows, 2 * group_rows), jnp.float32)],
        compiler_params=pltpu.CompilerParams(vmem_limit_bytes=vmem_bytes),
    )(grad_mid_full, attn_full, projected, probs)
    grad_rel_local = jnp.einsum(
        "hrt,brt->bh", diagonals, onehot, precision=lax.Precision.HIGHEST
    )
    grad_rel_full = lax.dynamic_update_slice_in_dim(
        jnp.zeros(rel_bias.shape, jnp.float32), grad_rel_local, head_start, 1
    )
    grad_one_local = line_sum(
        8, grad_one_sent.reshape(tensor_count, local_rows, model_width), "tensor"
    )
    grad_qkv_w = dot_tn(normed_one, grad_qkv)
    attn_grads = jnp.concatenate([grad_qkv_w, grad_out_w], axis=1).astype(bf)
    grad_in_norm, grad_gain_one = norm_backward(grad_one_local, input_f, scale_one, gain_attn)
    grad_tokens = (grad_middle + grad_in_norm).astype(bf)
    small = jnp.concatenate(
        [
            grad_gain_one,
            grad_gain_two,
            grad_rel_full.reshape(-1),
            grad_router_part.T.reshape(-1),
        ]
    )
    small_size = small.shape[0]
    small_rows = (small_size + 1023) // 1024 * 8
    small = jnp.pad(small, (0, small_rows * 128 - small_size)).reshape(small_rows, 128)
    (small_parts,) = exchange(9, [(small, "tensor", "gather")])
    small_parts, attn_back_parts = exchange(
        10,
        [
            (jnp.sum(small_parts, axis=0), "dp", "gather"),
            (attn_grads.reshape(group_count, width_share, 4 * head_width), "dp", "swap"),
        ],
    )
    small_sum = jnp.sum(small_parts, axis=0).reshape(-1)
    gain_one_sum = small_sum[:model_width]
    gain_two_sum = small_sum[model_width : 2 * model_width]
    rel_end = 2 * model_width + rel_bias.size
    rel_sum = small_sum[2 * model_width : rel_end].reshape(rel_bias.shape)
    router_whole = small_sum[rel_end : rel_end + expert_count * model_width].reshape(
        expert_count, model_width
    )
    router_sum = lax.dynamic_slice_in_dim(
        router_whole, lax.axis_index("dp") * width_share, width_share, 1
    ).T
    attn_sum = sum_parts(attn_back_parts)
    query_sum, key_sum, value_sum = (
        attn_sum[:, part * head_width : (part + 1) * head_width] for part in range(3)
    )
    out_sum = attn_sum[:, 3 * head_width :].T
    return (
        layer_out,
        grad_tokens,
        query_sum,
        key_sum,
        value_sum,
        out_sum,
        gain_one_sum,
        gain_two_sum,
        rel_sum,
        router_sum,
        inner_sum,
        outer_sum,
    )


def solution(mesh):
    return jax.shard_map(
        body,
        mesh=mesh,
        in_specs=(
            P(("dp", "tensor"), None),
            P("dp"),
            P("dp", None),
            P(("dp", "tensor"), None),
            P("dp", "tensor"),
            P("dp", "tensor"),
            P("dp", "tensor"),
            P("tensor", "dp"),
            P(),
            P(),
            P(),
            P("dp", None),
            P(None, "dp", "tensor"),
            P(None, "tensor", "dp"),
        ),
        out_specs=(
            P(("dp", "tensor"), None),
            P(("dp", "tensor"), None),
            P("dp", "tensor"),
            P("dp", "tensor"),
            P("dp", "tensor"),
            P("tensor", "dp"),
            P(),
            P(),
            P(),
            P("dp", None),
            P(None, "dp", "tensor"),
            P(None, "tensor", "dp"),
        ),
        check_vma=False,
    )
```

profile of v0, /device:TPU:0, one launch (start us, length us, event | category | flops | bytes accessed | tf_op | source)
XLA Modules:
  0.0 363.1 jit_solution(18222981529216297156)
XLA Ops:
  2.1 1.7 broadcast_in_dim.16
  3.8 5.3 %all-to-all-start = ((bf16[8,2,96,768]{3,2,1,0:T(8,128)(2,1)}), bf16[8,2,96,768]{3,2,1,0:T(8,128)(2,1)}, u32[]{:S(2)}, u32[]{:S(2)}) async-start(bf16[8,2,96,768]{3,2,1,0:T(8,128)(2,1)} %bitcast.15), calls=%async_computation | async-start | bytes 4718592 | tf_op jit(solution)/shard_map/all_to_all | solution.py:439
  12.5 40.5 %shard_map.247 = (bf16[4,128,768]{2,1,0:T(8,128)(2,1)}, bf16[8,96,896]{2,1,0:T(8,128)(2,1)}) custom-call(bf16[128,768]{1,0:T(8,128)(2,1)} %fusion.26.refs_0_, bf16[96,896]{1,0:T(8,128)(2,1)} %concatenate.17.refs_1_), custom_call_target="tpu_custom_call" | custom-call | tf_op jit(solution)/shard_map/pallas_call | solution.py:342
  53.0 2.4 copy.77
  56.6 5.5 %shard_map.248 = (bf16[512,576]{1,0:T(8,128)(2,1)S(1)}, f32[3,512,512]{2,1,0:T(8,128)}, bf16[512,192]{1,0:T(8,128)(2,1)S(1)}, bf16[512,768]{1,0:T(8,128)(2,1)S(1)}) custom-call(bf16[512,768]{1,0:T(8,128)(2,1)S(1)} %bitcast.88, bf16[768,896]{1,0:T(8,128)(2,1)S(1)} %bitcast.81, f32[3,8,1024]{2,1,0:T(8,128)S(1)} %copy.72.base_ref, s32[512,1]{1,0:T(8,128)S(1)} %copy.73.doc_col, ...), custom_call_target="tpu_custom_call" | custom-call | tf_op jit(solution)/shard_map/pallas_call | solution.py:448
  62.1 34.4 %shard_map.249 = f32[128,768]{1,0:T(8,128)S(1)} custom-call(bf16[4,128,768]{2,1,0:T(8,128)(2,1)S(1)} %bitcast.90), custom_call_target="tpu_custom_call" | custom-call | tf_op jit(solution)/shard_map/pallas_call | solution.py:194
  97.9 30.8 %shard_map.250 = (bf16[4,128,768]{2,1,0:T(8,128)(2,1)}, bf16[4,128,768]{2,1,0:T(8,128)(2,1)}) custom-call(bf16[128,768]{1,0:T(8,128)(2,1)} %multiply_convert_fusion.1.refs_0_, bf16[128,768]{1,0:T(8,128)(2,1)} %refs_1_.1), custom_call_target="tpu_custom_call" | custom-call | tf_op jit(solution)/shard_map/pallas_call | solution.py:342
  128.7 1.6 fusion.52
  131.0 2.5 convolution_convert_fusion
  133.5 28.4 %shard_map.251 = bf16[8,80,1536]{2,1,0:T(8,128)(2,1)} custom-call(bf16[8,80,1536]{2,1,0:T(8,128)(2,1)} %bitcast.100), custom_call_target="tpu_custom_call" | custom-call | tf_op jit(solution)/shard_map/pallas_call | solution.py:342
  161.9 1.9 fusion.51
  165.1 1.8 fusion.6
  168.3 2.3 convolution_convert_fusion.2
  170.6 2.1 convolution_convert_fusion.3
  173.7 1.5 pad_maximum_fusion.1
  175.1 26.0 %shard_map.252 = bf16[8,80,1536]{2,1,0:T(8,128)(2,1)} custom-call(bf16[8,80,1536]{2,1,0:T(8,128)(2,1)} %bitcast.94), custom_call_target="tpu_custom_call" | custom-call | tf_op jit(solution)/shard_map/pallas_call | solution.py:342
  201.2 3.0 convolution_convert_fusion.1
  204.2 40.5 %shard_map.253 = f32[128,1536]{1,0:T(8,128)S(1)} custom-call(bf16[4,128,1536]{2,1,0:T(8,128)(2,1)S(1)} %bitcast.89), custom_call_target="tpu_custom_call" | custom-call | tf_op jit(solution)/shard_map/pallas_call | solution.py:194
  245.5 1.7 multiply_reduce_fusion
  248.0 1.6 pad_maximum_fusion
  249.6 4.5 %all-to-all-start.1 = ((bf16[8,2,96,768]{3,2,1,0:T(8,128)(2,1)}), bf16[8,2,96,768]{3,2,1,0:T(8,128)(2,1)}, u32[]{:S(2)}, u32[]{:S(2)}) async-start(bf16[8,2,96,768]{3,2,1,0:T(8,128)(2,1)} %pad_maximum_fusion), calls=%async_computation.1 | async-start | bytes 4718592 | tf_op jit(solution)/shard_map/all_to_all | solution.py:515
  254.1 1.8 fusion.49
  256.0 19.9 %shard_map.254 = bf16[4,128,768]{2,1,0:T(8,128)(2,1)} custom-call(bf16[128,768]{1,0:T(8,128)(2,1)} %get-tuple-element.90.refs_0_), custom_call_target="tpu_custom_call" | custom-call | tf_op jit(solution)/shard_map/pallas_call | solution.py:342
  277.0 6.0 %shard_map.255 = (bf16[512,576]{1,0:T(8,128)(2,1)S(1)}, bf16[512,768]{1,0:T(8,128)(2,1)S(1)}, f32[3,8,1024]{2,1,0:T(8,128)S(1)}) custom-call(bf16[512,768]{1,0:T(8,128)(2,1)S(1)} %bitcast.85, bf16[768,896]{1,0:T(8,128)(2,1)S(1)} %bitcast.84, bf16[512,576]{1,0:T(8,128)(2,1)S(1)} %get-tuple-element.30.proj_ref, f32[3,512,512]{2,1,0:T(8,128)} %get-tuple-element.31.prob_ref), custom_call_target="tpu_custom_call" | custom-call | tf_op jit(solution)/shard_map/pallas_call | solution.py:560
  283.1 34.1 %shard_map.256 = f32[128,768]{1,0:T(8,128)S(1)} custom-call(bf16[4,128,768]{2,1,0:T(8,128)(2,1)S(1)} %bitcast.91), custom_call_target="tpu_custom_call" | custom-call | tf_op jit(solution)/shard_map/pallas_call | solution.py:194
  319.4 7.9 %shard_map.257 = f32[4,40,128]{2,1,0:T(8,128)} custom-call(f32[40,128]{1,0:T(8,128)} %fusion.39.refs_0_), custom_call_target="tpu_custom_call" | custom-call | tf_op jit(solution)/shard_map/pallas_call | solution.py:342
  327.3 1.5 reduce_sum.136.refs_0_
  329.5 1.9 convolution_convert_fusion.6
  332.6 19.7 %shard_map.258 = (f32[8,40,128]{2,1,0:T(8,128)}, bf16[8,96,768]{2,1,0:T(8,128)(2,1)}) custom-call(f32[40,128]{1,0:T(8,128)} %reduce_sum.136.refs_0_, bf16[8,96,768]{2,1,0:T(8,128)(2,1)} %pad_maximum_fusion.3.refs_1_), custom_call_target="tpu_custom_call" | custom-call | tf_op jit(solution)/shard_map/pallas_call | solution.py:342
  354.1 1.5 convert_reduce_fusion.1
  359.2 2.3 convert_reduce_fusion
  361.5 1.6 slice_bitcast_fusion
  (118 shorter events, 23.6 us)
Async XLA Ops:
  0.6 9.4 %copy-start = (f32[32,12]{0,1:T(8,128)S(1)}, f32[32,12]{0,1:T(8,128)}, u32[]{:S(2)}) copy-start(f32[32,12]{0,1:T(8,128)} %param.26) | copy-start | bytes 4612
  3.8 5.4 %copy-start.6 = (bf16[128,768]{1,0:T(8,128)(2,1)S(1)}, bf16[128,768]{1,0:T(8,128)(2,1)}, u32[]{:S(2)}) copy-start(bf16[128,768]{1,0:T(8,128)(2,1)} %param.16) | copy-start | bytes 589828
  3.8 6.0 %copy-start.30 = (bf16[96,4]{0,1:T(4,128)(2,1)S(1)}, bf16[96,4]{0,1:T(4,128)(2,1)}, u32[]{:S(2)}) copy-start(bf16[96,4]{0,1:T(4,128)(2,1)} %param.27) | copy-start | bytes 2308
  3.8 6.1 %copy-start.20 = (bf16[192,96]{1,0:T(8,128)(2,1)S(1)}, bf16[192,96]{1,0:T(8,128)(2,1)}, u32[]{:S(2)}) copy-start(bf16[192,96]{1,0:T(8,128)(2,1)} %param.23) | copy-start | bytes 110596
  3.8 6.3 %copy-start.7 = (f32[32,8,1024]{2,0,1:T(8,128)S(1)}, f32[32,8,1024]{2,0,1:T(8,128)}, u32[]{:S(2)}) copy-start(f32[32,8,1024]{2,0,1:T(8,128)} %constant.79.clone) | copy-start | bytes 3145732
  3.8 7.0 %copy-start.5 = (s32[512]{0:T(512)S(1)}, s32[512]{0:T(512)}, u32[]{:S(2)}) copy-start(s32[512]{0:T(512)} %param.17) | copy-start | bytes 6148
  3.8 158.2 %all-to-all-start = ((bf16[8,2,96,768]{3,2,1,0:T(8,128)(2,1)}), bf16[8,2,96,768]{3,2,1,0:T(8,128)(2,1)}, u32[]{:S(2)}, u32[]{:S(2)}) async-start(bf16[8,2,96,768]{3,2,1,0:T(8,128)(2,1)} %bitcast.15), calls=%async_computation | async-start | bytes 4718592 | tf_op jit(solution)/shard_map/all_to_all | solution.py:439
  9.1 2.6 copy-start.17
  9.1 2.6 copy-start.18
  9.1 2.6 copy-start.19
  9.8 45.7 %copy-start.26 = (f32[128]{0:T(128)}, f32[128]{0:T(128)S(1)}, u32[]{:S(2)}) copy-start(f32[128]{0:T(128)S(1)} %get-tuple-element.109) | copy-start | bytes 1540
  53.0 2.4 copy-start.1
  56.6 40.5 %copy-start.22 = (f32[768]{0:T(1024)S(1)}, f32[768]{0:T(1024)}, u32[]{:S(2)}) copy-start(f32[768]{0:T(1024)} %param.25) | copy-start | bytes 9220
  62.1 68.3 %copy-start.24 = (s32[512,1]{0,1:T(1,128)S(1)}, s32[512,1]{0,1:T(1,128)}, u32[]{:S(2)}) copy-start(s32[512,1]{0,1:T(1,128)} %param.18) | copy-start | bytes 6148
  62.1 68.4 %copy-start.16 = (bf16[512,512]{1,0:T(8,128)(2,1)S(1)}, bf16[512,512]{1,0:T(8,128)(2,1)}, u32[]{:S(2)}) copy-start(bf16[512,512]{1,0:T(8,128)(2,1)} %constant.80.clone) | copy-start | bytes 1572868
  97.1 148.4 %copy-start.28 = (f32[128]{0:T(128)}, f32[128]{0:T(128)S(1)}, u32[]{:S(2)}) copy-start(f32[128]{0:T(128)S(1)} %get-tuple-element.111) | copy-start | bytes 1540
  128.7 2.1 copy-start.14
  128.7 2.3 copy-start.15
  161.9 2.3 copy-start.9
  204.2 40.5 %copy-start.11 = (bf16[128,768]{1,0:T(8,128)(2,1)S(1)}, bf16[128,768]{1,0:T(8,128)(2,1)}, u32[]{:S(2)}) copy-start(bf16[128,768]{1,0:T(8,128)(2,1)} %refs_1_.1) | copy-start | bytes 589828
  204.2 43.0 %copy-start.10 = (bf16[128,768]{1,0:T(8,128)(2,1)S(1)}, bf16[128,768]{1,0:T(8,128)(2,1)}, u32[]{:S(2)}) copy-start(bf16[128,768]{1,0:T(8,128)(2,1)} %multiply_convert_fusion.1.refs_0_) | copy-start | bytes 589828
  244.7 3.3 copy-start.12
  244.7 3.2 copy-start.13
  249.6 4.5 %copy-start.29 = (f32[128]{0:T(128)S(1)}, f32[128]{0:T(128)}, u32[]{:S(2)}) copy-start(f32[128]{0:T(128)} %copy-done.28) | copy-start | bytes 1540
  249.6 4.5 %copy-start.32 = (f32[128]{0:T(128)S(1)}, f32[128]{0:T(128)}, u32[]{:S(2)}) copy-start(f32[128]{0:T(128)} %get-tuple-element.110) | copy-start | bytes 1540
  249.6 109.6 %all-to-all-start.1 = ((bf16[8,2,96,768]{3,2,1,0:T(8,128)(2,1)}), bf16[8,2,96,768]{3,2,1,0:T(8,128)(2,1)}, u32[]{:S(2)}, u32[]{:S(2)}) async-start(bf16[8,2,96,768]{3,2,1,0:T(8,128)(2,1)} %pad_maximum_fusion), calls=%async_computation.1 | async-start | bytes 4718592 | tf_op jit(solution)/shard_map/all_to_all | solution.py:515
  277.0 40.2 %copy-start.8 = (f32[32,8,1024]{2,0,1:T(8,128)S(1)}, f32[32,8,1024]{2,0,1:T(8,128)}, u32[]{:S(2)}) copy-start(f32[32,8,1024]{2,0,1:T(8,128)} %constant.79.clone) | copy-start | bytes 3145732
  283.0 35.2 %copy-start.27 = (f32[128]{0:T(128)S(1)}, f32[128]{0:T(128)}, u32[]{:S(2)}) copy-start(f32[128]{0:T(128)} %copy-done.26) | copy-start | bytes 1540
  283.1 35.3 %copy-start.21 = (f32[4,768]{1,0:T(4,128)S(1)}, f32[4,768]{1,0:T(4,128)}, u32[]{:S(2)}) copy-start(f32[4,768]{1,0:T(4,128)} %fusion.53) | copy-start | bytes 36868
  283.1 35.7 %copy-start.25 = (f32[768]{0:T(1024)S(1)}, f32[768]{0:T(1024)}, u32[]{:S(2)}) copy-start(f32[768]{0:T(1024)} %get-tuple-element.86) | copy-start | bytes 9220
  283.1 45.7 %copy-start.3 = (bf16[4,128,768]{2,1,0:T(8,128)(2,1)S(1)}, bf16[4,128,768]{2,1,0:T(8,128)(2,1)}, u32[]{:S(2)}) copy-start(bf16[4,128,768]{2,1,0:T(8,128)(2,1)} %shard_map.254) | copy-start | bytes 2359300
  332.6 25.7 %copy-start.31 = (f32[128]{0:T(128)S(1)}, f32[128]{0:T(128)}, u32[]{:S(2)}) copy-start(f32[128]{0:T(128)} %get-tuple-element.108) | copy-start | bytes 1540
  (3 other events, 4.1 us)
where the time goes:
time: 364 us; the launch traced here: 363 us
  Pallas kernels  294 us (81%)
  matrix products  23 us (6%)
  other arithmetic  19.4 us (5%)
  local copies, waits for them, and re-layouts  15.9 us (4%)
  starting transfers between devices  9.82 us (3%)
    pallas_call x7, Pallas kernels, exchange(): pl.pallas_call(functools.partial(exchange_kernel, plan, sizes), out_shape...  173 us
    pallas_call x3, Pallas kernels, line_sum(): pl.pallas_call(functools.partial(line_sum_kernel, axis, size), out_shape=...  109 us
    dot_general x5, matrix products, dot_tn(): lax.dot_general(left, right, (((0,), (0,)), ((), ())), preferred_element_...  9.7 us
  transfers between devices with their start and end apart: 2, of which 0 were waited for; matrix products, arithmetic and copies ran while one was open for 8% of the time, Pallas kernels for 63%

commit v1 on v0

--- a/solution.py
+++ b/solution.py
@@ -125,11 +125,52 @@
                     hop(way, step, piece).wait_send()
 
 
-def line_sum_kernel(axis, size, x_ref, out_ref, got, going, send_sem, recv_sem):
+def greet_direct(barrier, axis, size):
+    me = lax.axis_index(axis)
+    for step in range(1, size):
+        pl.semaphore_signal(
+            barrier,
+            inc=1,
+            device_id={axis: lax.rem(me + step, size)},
+            device_id_type=pl.DeviceIdType.MESH,
+        )
+    return size - 1
+
+
+def start_swap(axis, size, x_ref, out_ref, send_sem, recv_sem):
+    me = lax.axis_index(axis)
+    copies = []
+    for step in range(1, size):
+        peer = lax.rem(me + step, size)
+        copy = pltpu.make_async_remote_copy(
+            src_ref=x_ref.at[peer],
+            dst_ref=out_ref.at[me],
+            send_sem=send_sem.at[step],
+            recv_sem=recv_sem.at[step],
+            device_id={axis: peer},
+            device_id_type=pl.DeviceIdType.MESH,
+        )
+        copy.start()
+        copies.append(copy)
+    own = pltpu.make_async_copy(x_ref.at[me], out_ref.at[me], send_sem.at[0])
+    own.start()
+    return copies + [own]
+
+
+def line_sum_kernel(axis, size, beside, *refs):
+    x_ref = refs[0]
+    if beside:
+        other_ref, out_ref, other_out, got, going, send_sem, recv_sem, swap_send, swap_recv = refs[1:]
+    else:
+        out_ref, got, going, send_sem, recv_sem = refs[1:]
     me = lax.axis_index(axis)
     barrier = pltpu.get_barrier_semaphore()
-    pl.semaphore_wait(barrier, greet_line(barrier, axis, size))
+    greeted = greet_line(barrier, axis, size)
+    if beside:
+        greeted += greet_direct(barrier, *beside)
+    pl.semaphore_wait(barrier, greeted)
     rows = x_ref.shape[1] // pieces
+    far = (me >= size // 2).astype(jnp.int32)
 
     def hop(way, dest, piece):
         part = pl.ds(piece * rows, rows)
@@ -143,15 +184,17 @@
         )
 
     def before(way, dest):
-        return me < dest if way == 0 else me > dest
+        return (1 - 2 * way) * (dest - me) > 0
 
     def first(way):
-        return me == 0 if way == 0 else me == size - 1
-
-    for order in range(size - 1):
-        for piece in range(pieces):
-            for way in range(2):
-                dest = size - 1 - order if way == 0 else order
+        return me == (size - 1) * way
+
+    copies = []
+    for turn in range(2):
+        way = far if turn == 0 else 1 - far
+        for order in range(size - 1):
+            dest = (size - 1 - order) * (1 - way) + order * way
+            for piece in range(pieces):
                 part = pl.ds(piece * rows, rows)
 
                 @pl.when(before(way, dest) & first(way))
@@ -170,6 +213,9 @@
                 def send(way=way, dest=dest, piece=piece):
                     hop(way, dest, piece).start()
 
+        if beside and turn == 0:
+            copies = start_swap(*beside, other_ref, other_out, swap_send, swap_recv)
+
     out_ref[...] = x_ref[me].astype(jnp.float32)
     for way in range(2):
 
@@ -187,25 +233,38 @@
                 def gone(way=way, dest=dest, piece=piece):
                     hop(way, dest, piece).wait_send()
 
-
-def line_sum(ident, x, axis):
+    for copy in copies:
+        copy.wait()
+
+
+def line_sum(ident, x, axis, other=None, other_axis=None):
     size = lax.axis_size(axis)
     block = pl.BlockSpec(memory_space=pltpu.VMEM)
+    place = pl.BlockSpec(memory_space=pl.ANY)
+    out_shape = [jax.ShapeDtypeStruct(x.shape[1:], jnp.float32)]
+    scratch = [
+        pltpu.VMEM((2,) + x.shape, x.dtype),
+        pltpu.VMEM((2,) + x.shape, x.dtype),
+        pltpu.SemaphoreType.DMA((2, size, pieces)),
+        pltpu.SemaphoreType.DMA((2, size, pieces)),
+    ]
+    beside = None
+    extra = []
+    if other is not None:
+        beside = (other_axis, lax.axis_size(other_axis))
+        extra = [other]
+        out_shape.append(jax.ShapeDtypeStruct(other.shape, other.dtype))
+        scratch += [pltpu.SemaphoreType.DMA((beside[1],)), pltpu.SemaphoreType.DMA((beside[1],))]
     return pl.pallas_call(
-        functools.partial(line_sum_kernel, axis, size),
-        out_shape=jax.ShapeDtypeStruct(x.shape[1:], jnp.float32),
-        in_specs=[block],
-        out_specs=block,
-        scratch_shapes=[
-            pltpu.VMEM((2,) + x.shape, x.dtype),
-            pltpu.VMEM((2,) + x.shape, x.dtype),
-            pltpu.SemaphoreType.DMA((2, size, pieces)),
-            pltpu.SemaphoreType.DMA((2, size, pieces)),
-        ],
+        functools.partial(line_sum_kernel, axis, size, beside),
+        out_shape=out_shape,
+        in_specs=[block] + [place] * len(extra),
+        out_specs=[block] + [place] * len(extra),
+        scratch_shapes=scratch,
         compiler_params=pltpu.CompilerParams(
             collective_id=ident, has_side_effects=True, vmem_limit_bytes=vmem_bytes
         ),
-    )(x)
+    )(x, *extra)
 
 
 def attend_kernel(head_width, normed_ref, weights_ref, base_ref, doc_col, doc_row, proj_ref, prob_ref, mixed_ref, sent_ref, bias):
@@ -433,9 +492,16 @@
     input_f = tokens.astype(jnp.float32)
     scale_one = rms_scale(input_f)
     sent_one = (input_f * scale_one * gain_attn).astype(bf)
-    normed_parts, attn_parts = exchange(
-        1, [(sent_one, "tensor", "line"), (sent_attn, "dp", "gather")]
-    )
+    normed_parts, attn_parts, grad_full = exchange(
+        1,
+        [
+            (sent_one, "tensor", "line"),
+            (sent_attn, "dp", "gather"),
+            (cotangent, "tensor", "line"),
+        ],
+    )
+    grad_full = grad_full.reshape(group_rows, model_width)
+    sent_experts, normed_parts = lax.optimization_barrier((sent_experts, normed_parts))
     expert_parts = lax.all_to_all(sent_experts, "dp", split_axis=0, concat_axis=0, tiled=True)
     normed_one = normed_parts.reshape(group_rows, model_width)
     attn_full = attn_parts.reshape(model_width, sent_attn.shape[1])
@@ -458,21 +524,10 @@
         scratch_shapes=[pltpu.VMEM((group_rows, group_rows), jnp.float32)],
         compiler_params=pltpu.CompilerParams(vmem_limit_bytes=vmem_bytes),
     )(normed_one, attn_full, rel_base, doc_ids[:, None], doc_ids[None, :])
-    attn_sum_local = line_sum(
+    (attn_sum_local,) = line_sum(
         2, attn_sent.reshape(tensor_count, local_rows, model_width), "tensor"
     )
-    middle = input_f + attn_sum_local
-    scale_two = rms_scale(middle)
-    normed_local = (middle * scale_two * gain_expert).astype(bf)
-    normed_two, grad_full = exchange(
-        3, [(normed_local, "tensor", "line"), (cotangent, "tensor", "line")]
-    )
-    normed_two = normed_two.reshape(group_rows, model_width)
-    grad_full = grad_full.reshape(group_rows, model_width)
-    logits = dot_nn(normed_two, router_full)
-    gate_probs = jax.nn.softmax(logits, axis=-1)
     chosen = route_ids[:, None] == jnp.arange(expert_count)[None, :]
-    gate_value = jnp.sum(jnp.where(chosen, gate_probs, 0.0), axis=-1)
     earlier = jnp.asarray(np.tril(np.ones((group_rows, group_rows), np.float32), -1), bf)
     counts = dot_nn(earlier, chosen.astype(bf))
     slot_index = jnp.sum(jnp.where(chosen, counts, 0.0), axis=-1).astype(jnp.int32)
@@ -481,15 +536,36 @@
     place = (
         slot_place[None, :] == jnp.arange(group_count * share_pad, dtype=jnp.int32)[:, None]
     ).astype(bf)
-    grad_f = grad_full.astype(jnp.float32)
-    gated = (gate_value[:, None] * grad_f).astype(bf)
-    both = dot_nn(place, jnp.concatenate([normed_two, gated], axis=1)).astype(bf)
-    (recv_both,) = exchange(
-        4, [(both.reshape(group_count, share_pad, 2 * model_width), "dp", "swap")]
-    )
-    recv_both = recv_both.reshape(group_count * share_pad, 2 * model_width)
-    rows_mine = recv_both[:, :model_width]
-    grad_mine = recv_both[:, model_width:]
+    grad_slots = dot_nn(place, grad_full).astype(bf)
+    middle = input_f + attn_sum_local
+    scale_two = rms_scale(middle)
+    normed_local = (middle * scale_two * gain_expert).astype(bf)
+    normed_two, recv_grad = exchange(
+        3,
+        [
+            (normed_local, "tensor", "line"),
+            (grad_slots.reshape(group_count, share_pad, model_width), "dp", "swap"),
+        ],
+    )
+    normed_two = normed_two.reshape(group_rows, model_width)
+    logits = dot_nn(normed_two, router_full)
+    gate_probs = jax.nn.softmax(logits, axis=-1)
+    gate_value = jnp.sum(jnp.where(chosen, gate_probs, 0.0), axis=-1)
+    gate_slots = jnp.sum(jnp.where(place > 0, gate_value[None, :], 0.0), axis=1)
+    sent_rows = dot_nn(place, normed_two).astype(bf)
+    recv_rows, recv_gate = exchange(
+        4,
+        [
+            (sent_rows.reshape(group_count, share_pad, model_width), "dp", "swap"),
+            (gate_slots.reshape(group_count, 1, share_pad), "dp", "swap"),
+        ],
+    )
+    rows_mine = recv_rows.reshape(group_count * share_pad, model_width)
+    grad_mine = (
+        (recv_gate.reshape(group_count, share_pad, 1) * recv_grad.astype(jnp.float32))
+        .astype(bf)
+        .reshape(group_count * share_pad, model_width)
+    )
     inner_mine = expert_parts[:, 0].reshape(model_width, hidden_share)
     outer_mine = expert_parts[:, 1].reshape(model_width, hidden_share)
     inner_pre = dot_nn(rows_mine, inner_mine)
@@ -498,17 +574,22 @@
     expert_part = dot_nt(inner_act, outer_mine).astype(bf)
     grad_pre = gelu_pull(dot_nn(grad_mine, outer_mine))[0].astype(bf)
     grad_rows = dot_nt(grad_pre, inner_mine).astype(bf)
-    (back_both,) = exchange(
-        5,
-        [
-            (
-                jnp.concatenate([expert_part, grad_rows], axis=1).reshape(
-                    group_count, share_pad, 2 * model_width
-                ),
-                "dp",
-                "swap",
-            )
-        ],
+    (back_rows,) = exchange(
+        5, [(expert_part.reshape(group_count, share_pad, model_width), "dp", "swap")]
+    )
+    returned = dot_tn(place, back_rows.reshape(group_count * share_pad, model_width)).astype(bf)
+    expert_local, back_grads = line_sum(
+        6,
+        returned.reshape(tensor_count, local_rows, model_width),
+        "tensor",
+        grad_rows.reshape(group_count, share_pad, model_width),
+        "dp",
+    )
+    grads_returned = dot_tn(
+        place, back_grads.reshape(group_count * share_pad, model_width)
+    ).astype(bf)
+    (slots_local,) = line_sum(
+        11, grads_returned.reshape(tensor_count, local_rows, model_width), "tensor"
     )
     inner_grad = dot_tn(rows_mine, grad_pre).astype(bf)
     outer_grad = dot_tn(grad_mine, inner_act).astype(bf)
@@ -533,9 +614,6 @@
     )
     inner_sum = weight_sum[:, 0]
     outer_sum = weight_sum[:, 1].transpose(0, 2, 1)
-    returned = dot_tn(place, back_both.reshape(group_count * share_pad, 2 * model_width)).astype(bf)
-    row_sum = line_sum(6, returned.reshape(tensor_count, local_rows, 2 * model_width), "tensor")
-    expert_local = row_sum[:, :model_width]
     gate_local = lax.dynamic_slice_in_dim(gate_value, my_start, local_rows, 0)
     layer_out = (middle + gate_local[:, None] * expert_local).astype(bf)
     cot_local = cotangent.astype(jnp.float32)
@@ -551,7 +629,7 @@
     router_term = jnp.einsum(
         "qe,de->qd", grad_logits, router_full, preferred_element_type=jnp.float32
     )
-    grad_two_local = row_sum[:, model_width:] + router_term
+    grad_two_local = slots_local + router_term
     grad_mid, grad_gain_two = norm_backward(grad_two_local, middle, scale_two, gain_expert)
     grad_middle = cot_local + grad_mid
     (grad_mid_full,) = exchange(7, [(grad_middle.astype(bf), "tensor", "line")])
@@ -575,11 +653,15 @@
     grad_rel_full = lax.dynamic_update_slice_in_dim(
         jnp.zeros(rel_bias.shape, jnp.float32), grad_rel_local, head_start, 1
     )
-    grad_one_local = line_sum(
-        8, grad_one_sent.reshape(tensor_count, local_rows, model_width), "tensor"
-    )
     grad_qkv_w = dot_tn(normed_one, grad_qkv)
     attn_grads = jnp.concatenate([grad_qkv_w, grad_out_w], axis=1).astype(bf)
+    grad_one_local, attn_back_parts = line_sum(
+        8,
+        grad_one_sent.reshape(tensor_count, local_rows, model_width),
+        "tensor",
+        attn_grads.reshape(group_count, width_share, 4 * head_width),
+        "dp",
+    )
     grad_in_norm, grad_gain_one = norm_backward(grad_one_local, input_f, scale_one, gain_attn)
     grad_tokens = (grad_middle + grad_in_norm).astype(bf)
     small = jnp.concatenate(
@@ -594,13 +676,7 @@
     small_rows = (small_size + 1023) // 1024 * 8
     small = jnp.pad(small, (0, small_rows * 128 - small_size)).reshape(small_rows, 128)
     (small_parts,) = exchange(9, [(small, "tensor", "gather")])
-    small_parts, attn_back_parts = exchange(
-        10,
-        [
-            (jnp.sum(small_parts, axis=0), "dp", "gather"),
-            (attn_grads.reshape(group_count, width_share, 4 * head_width), "dp", "swap"),
-        ],
-    )
+    (small_parts,) = exchange(10, [(jnp.sum(small_parts, axis=0), "dp", "gather")])
     small_sum = jnp.sum(small_parts, axis=0).reshape(-1)
     gain_one_sum = small_sum[:model_width]
     gain_two_sum = small_sum[model_width : 2 * model_width]

time: 364 us -> 296 us (0.81)
  Pallas kernels: 294 us -> 226 us
    pallas_call x7, Pallas kernels: 173 us -> 117 us  [exchange(): pl.pallas_call(functools.partial(exchange_kernel, plan, sizes), out_shape...]
    pallas_call x3 -> x4, Pallas kernels: 109 us -> 98 us  [line_sum(): pl.pallas_call(functools.partial(line_sum_kernel, axis, size, beside), ou...]
    dot_general x5 -> x6, matrix products: 7.04 us -> 9.07 us  [dot_nn(): return jnp.dot(left, right, preferred_element_type=jnp.float32)]
    dot_general x5 -> x6, matrix products: 9.7 us -> 9.72 us  [dot_tn(): lax.dot_general(left, right, (((0,), (0,)), ((), ())), preferred_element_...]
  transfers between devices with their start and end apart: 2 -> 2, of which waited for: 0 -> 0; matrix products, arithmetic and copies ran while one was open for 8% -> 8% of each run, Pallas kernels for 63% -> 37%
where the time goes in v1:
time: 296 us; the launch traced here: 295 us
  Pallas kernels  226 us (76%)
  matrix products  25.5 us (9%)
  other arithmetic  16.4 us (6%)
  local copies, waits for them, and re-layouts  16.3 us (6%)
  starting transfers between devices  9 us (3%)
    pallas_call x7, Pallas kernels, exchange(): pl.pallas_call(functools.partial(exchange_kernel, plan, sizes), out_shape...  117 us
    pallas_call x4, Pallas kernels, line_sum(): pl.pallas_call(functools.partial(line_sum_kernel, axis, size, beside), ou...  98 us
    dot_general x6, matrix products, dot_tn(): lax.dot_general(left, right, (((0,), (0,)), ((), ())), preferred_element_...  9.72 us
    dot_general x6, matrix products, dot_nn(): return jnp.dot(left, right, preferred_element_type=jnp.float32)  9.07 us
    pallas_call x1, Pallas kernels, body(): pl.pallas_call(functools.partial(attend_back_kernel, head_width), out_sha...  6.03 us
  transfers between devices with their start and end apart: 2, of which 0 were waited for; matrix products, arithmetic and copies ran while one was open for 8% of the time, Pallas kernels for 37%

profile of v1, /device:TPU:0, one launch (start us, length us, event | category | flops | bytes accessed | tf_op | source)
XLA Modules:
  0.0 294.8 jit_solution(16901792907274355657)
XLA Ops:
  4.3 36.7 %shard_map.247 = (bf16[4,128,768]{2,1,0:T(8,128)(2,1)}, bf16[8,96,896]{2,1,0:T(8,128)(2,1)}, bf16[4,128,768]{2,1,0:T(8,128)(2,1)}) custom-call(bf16[128,768]{1,0:T(8,128)(2,1)} %fusion.17.refs_0_, bf16[96,896]{1,0:T(8,128)(2,1)} %concatenate.11.refs_1_, bf16[128,768]{1,0:T(8,128)(2,1)} %refs_2_.1), custom_call_target="tpu_custom_call" | custom-call | tf_op jit(solution)/shard_map/pallas_call | solution.py:401
  41.0 1.6 broadcast_in_dim.25
  42.7 4.5 %all-to-all-start = ((bf16[8,2,96,768]{3,2,1,0:T(8,128)(2,1)}), bf16[8,2,96,768]{3,2,1,0:T(8,128)(2,1)}, u32[]{:S(2)}, u32[]{:S(2)}) async-start(bf16[8,2,96,768]{3,2,1,0:T(8,128)(2,1)} %bitcast.108), calls=%async_computation | async-start | bytes 4718592 | tf_op jit(solution)/shard_map/all_to_all | solution.py:505
  47.2 1.9 fusion.37
  49.4 5.5 %shard_map.248 = (bf16[512,576]{1,0:T(8,128)(2,1)S(1)}, f32[3,512,512]{2,1,0:T(8,128)}, bf16[512,192]{1,0:T(8,128)(2,1)S(1)}, bf16[512,768]{1,0:T(8,128)(2,1)S(1)}) custom-call(bf16[512,768]{1,0:T(8,128)(2,1)S(1)} %bitcast.98, bf16[768,896]{1,0:T(8,128)(2,1)S(1)} %bitcast.92, f32[3,8,1024]{2,1,0:T(8,128)S(1)} %copy.88.base_ref, s32[512,1]{1,0:T(8,128)S(1)} %copy.89.doc_col, ...), custom_call_target="tpu_custom_call" | custom-call | tf_op jit(solution)/shard_map/pallas_call | solution.py:514
  54.9 17.4 %shard_map.249 = f32[128,768]{1,0:T(8,128)S(1)} custom-call(bf16[4,128,768]{2,1,0:T(8,128)(2,1)S(1)} %bitcast.102), custom_call_target="tpu_custom_call" | custom-call | tf_op jit(solution)/shard_map/pallas_call | solution.py:258
  73.6 1.6 convolution_convert_fusion.5
  75.2 19.2 %shard_map.250 = (bf16[4,128,768]{2,1,0:T(8,128)(2,1)}, bf16[8,80,768]{2,1,0:T(8,128)(2,1)}) custom-call(bf16[128,768]{1,0:T(8,128)(2,1)} %multiply_convert_fusion.2.refs_0_, bf16[8,80,768]{2,1,0:T(8,128)(2,1)} %bitcast.120), custom_call_target="tpu_custom_call" | custom-call | tf_op jit(solution)/shard_map/pallas_call | solution.py:401
  98.2 2.9 convolution_convert_fusion.4
  101.1 14.8 %shard_map.251 = (bf16[8,80,768]{2,1,0:T(8,128)(2,1)}, f32[8,1,80]{2,1,0:T(1,128)}) custom-call(bf16[8,80,768]{2,1,0:T(8,128)(2,1)} %bitcast.119, f32[8,1,80]{2,1,0:T(1,128)} %reshape.187.refs_1_), custom_call_target="tpu_custom_call" | custom-call | tf_op jit(solution)/shard_map/pallas_call | solution.py:401
  115.9 1.9 multiply_convert_fusion
  117.8 1.9 fusion.41
  120.9 1.9 fusion.6
  122.8 2.3 convolution_convert_fusion.3
  125.0 2.3 convolution_convert_fusion
  128.3 2.1 convolution_convert_fusion.1
  130.4 15.5 %shard_map.252 = bf16[8,80,768]{2,1,0:T(8,128)(2,1)} custom-call(bf16[8,80,768]{2,1,0:T(8,128)(2,1)} %bitcast.118), custom_call_target="tpu_custom_call" | custom-call | tf_op jit(solution)/shard_map/pallas_call | solution.py:401
  145.9 2.1 convolution_convert_fusion.8
  148.0 20.4 %shard_map.253 = (f32[128,768]{1,0:T(8,128)S(1)}, bf16[8,80,768]{2,1,0:T(8,128)(2,1)S(1)}) custom-call(bf16[4,128,768]{2,1,0:T(8,128)(2,1)S(1)} %bitcast.101, bf16[8,80,768]{2,1,0:T(8,128)(2,1)S(1)} %bitcast.100), custom_call_target="tpu_custom_call" | custom-call | tf_op jit(solution)/shard_map/pallas_call | solution.py:258
  169.4 23.0 %shard_map.254 = f32[128,768]{1,0:T(8,128)S(1)} custom-call(bf16[4,128,768]{2,1,0:T(8,128)(2,1)S(1)} %bitcast.103), custom_call_target="tpu_custom_call" | custom-call | tf_op jit(solution)/shard_map/pallas_call | solution.py:258
  194.2 16.6 %shard_map.255 = bf16[4,128,768]{2,1,0:T(8,128)(2,1)} custom-call(bf16[128,768]{1,0:T(8,128)(2,1)} %get-tuple-element.116.refs_0_), custom_call_target="tpu_custom_call" | custom-call | tf_op jit(solution)/shard_map/pallas_call | solution.py:401
  210.7 2.4 copy.92
  214.2 6.0 %shard_map.256 = (bf16[512,576]{1,0:T(8,128)(2,1)S(1)}, bf16[512,768]{1,0:T(8,128)(2,1)S(1)}, f32[3,8,1024]{2,1,0:T(8,128)S(1)}) custom-call(bf16[512,768]{1,0:T(8,128)(2,1)S(1)} %bitcast.97, bf16[768,896]{1,0:T(8,128)(2,1)S(1)} %bitcast.95, bf16[512,576]{1,0:T(8,128)(2,1)S(1)} %copy-done.5, f32[3,512,512]{2,1,0:T(8,128)} %get-tuple-element.45.prob_ref), custom_call_target="tpu_custom_call" | custom-call | tf_op jit(solution)/shard_map/pallas_call | solution.py:638
  221.8 2.9 pad_maximum_fusion
  224.7 4.5 %all-to-all-start.1 = ((bf16[8,2,96,768]{3,2,1,0:T(8,128)(2,1)}), bf16[8,2,96,768]{3,2,1,0:T(8,128)(2,1)}, u32[]{:S(2)}, u32[]{:S(2)}) async-start(bf16[8,2,96,768]{3,2,1,0:T(8,128)(2,1)} %pad_maximum_fusion), calls=%async_computation.1 | async-start | bytes 4718592 | tf_op jit(solution)/shard_map/all_to_all | solution.py:596
  229.6 1.9 convolution_convert_fusion.6
  231.7 37.2 %shard_map.257 = (f32[128,768]{1,0:T(8,128)S(1)}, bf16[8,96,768]{2,1,0:T(8,128)(2,1)S(1)}) custom-call(bf16[4,128,768]{2,1,0:T(8,128)(2,1)S(1)} %bitcast.104, bf16[8,96,768]{2,1,0:T(8,128)(2,1)S(1)} %pad_maximum_fusion.2.refs_1_), custom_call_target="tpu_custom_call" | custom-call | tf_op jit(solution)/shard_map/pallas_call | solution.py:258
  269.7 6.6 %shard_map.258 = f32[4,40,128]{2,1,0:T(8,128)} custom-call(f32[40,128]{1,0:T(8,128)} %fusion.30.refs_0_), custom_call_target="tpu_custom_call" | custom-call | tf_op jit(solution)/shard_map/pallas_call | solution.py:401
  276.3 1.5 reduce_sum.147.refs_0_
  277.8 7.5 %shard_map.259 = f32[8,40,128]{2,1,0:T(8,128)} custom-call(f32[40,128]{1,0:T(8,128)} %reduce_sum.147.refs_0_), custom_call_target="tpu_custom_call" | custom-call | tf_op jit(solution)/shard_map/pallas_call | solution.py:401
  290.9 2.3 convert_reduce_fusion
  293.2 1.6 slice_bitcast_fusion
  (114 shorter events, 23.0 us)
Async XLA Ops:
  0.6 46.5 %copy-start = (f32[32,12]{0,1:T(8,128)S(1)}, f32[32,12]{0,1:T(8,128)}, u32[]{:S(2)}) copy-start(f32[32,12]{0,1:T(8,128)} %param.26) | copy-start | bytes 4612
  0.7 1.6 copy-start.9
  0.7 1.7 copy-start.22
  0.7 1.8 copy-start.26
  0.7 1.9 copy-start.24
  2.1 1.3 copy-start.19
  2.1 1.3 copy-start.20
  2.1 1.3 copy-start.21
  42.6 6.6 %copy-start.6 = (s32[512]{0:T(512)S(1)}, s32[512]{0:T(512)}, u32[]{:S(2)}) copy-start(s32[512]{0:T(512)} %param.17) | copy-start | bytes 6148
  42.7 6.7 %copy-start.3 = (bf16[4,128,768]{2,1,0:T(8,128)(2,1)S(1)}, bf16[4,128,768]{2,1,0:T(8,128)(2,1)}, u32[]{:S(2)}) copy-start(bf16[4,128,768]{2,1,0:T(8,128)(2,1)} %get-tuple-element.33) | copy-start | bytes 2359300
  42.7 75.1 %all-to-all-start = ((bf16[8,2,96,768]{3,2,1,0:T(8,128)(2,1)}), bf16[8,2,96,768]{3,2,1,0:T(8,128)(2,1)}, u32[]{:S(2)}, u32[]{:S(2)}) async-start(bf16[8,2,96,768]{3,2,1,0:T(8,128)(2,1)} %bitcast.108), calls=%async_computation | async-start | bytes 4718592 | tf_op jit(solution)/shard_map/all_to_all | solution.py:505
  47.2 2.2 copy-start.1
  49.4 23.1 %copy-start.18 = (bf16[512,512]{1,0:T(8,128)(2,1)S(1)}, bf16[512,512]{1,0:T(8,128)(2,1)}, u32[]{:S(2)}) copy-start(bf16[512,512]{1,0:T(8,128)(2,1)} %constant.81.clone) | copy-start | bytes 1572868
  49.4 23.1 %copy-start.25 = (s32[512,1]{0,1:T(1,128)S(1)}, s32[512,1]{0,1:T(1,128)}, u32[]{:S(2)}) copy-start(s32[512,1]{0,1:T(1,128)} %param.18) | copy-start | bytes 6148
  54.9 20.3 %copy-start.4 = (bf16[512,576]{1,0:T(8,128)(2,1)}, bf16[512,576]{1,0:T(8,128)(2,1)S(1)}, u32[]{:S(2)}) copy-start(bf16[512,576]{1,0:T(8,128)(2,1)S(1)} %get-tuple-element.44.proj_ref) | copy-start | bytes 1769476
  54.9 17.9 %copy-start.23 = (f32[768]{0:T(1024)S(1)}, f32[768]{0:T(1024)}, u32[]{:S(2)}) copy-start(f32[768]{0:T(1024)} %param.25) | copy-start | bytes 9220
  54.9 18.6 %copy-start.28 = (bf16[4,128,768]{2,1,0:T(8,128)(2,1)S(1)}, bf16[4,128,768]{2,1,0:T(8,128)(2,1)}, u32[]{:S(2)}) copy-start(bf16[4,128,768]{2,1,0:T(8,128)(2,1)} %get-tuple-element.36) | copy-start | bytes 2359300
  98.2 17.6 %copy-start.16 = (bf16[8,80,768]{2,1,0:T(8,128)(2,1)S(1)}, bf16[8,80,768]{2,1,0:T(8,128)(2,1)}, u32[]{:S(2)}) copy-start(bf16[8,80,768]{2,1,0:T(8,128)(2,1)} %get-tuple-element.41) | copy-start | bytes 2949124
  117.7 1.9 copy-start.17
  119.7 1.2 copy-start.27
  168.4 24.0 %copy-start.12 = (bf16[128,768]{1,0:T(8,128)(2,1)S(1)}, bf16[128,768]{1,0:T(8,128)(2,1)}, u32[]{:S(2)}) copy-start(bf16[128,768]{1,0:T(8,128)(2,1)} %refs_2_.1) | copy-start | bytes 589828
  168.4 24.1 %copy-start.13 = (bf16[128,768]{1,0:T(8,128)(2,1)S(1)}, bf16[128,768]{1,0:T(8,128)(2,1)}, u32[]{:S(2)}) copy-start(bf16[128,768]{1,0:T(8,128)(2,1)} %multiply_convert_fusion.2.refs_0_) | copy-start | bytes 589828
  210.7 2.4 copy-start.2
  213.1 1.1 copy-start.5
  214.2 6.1 %copy-start.10 = (f32[32,8,1024]{2,0,1:T(8,128)S(1)}, f32[32,8,1024]{2,0,1:T(8,128)}, u32[]{:S(2)}) copy-start(f32[32,8,1024]{2,0,1:T(8,128)} %constant.80.clone) | copy-start | bytes 3145732
  220.3 1.0 copy-start.7
  220.3 1.5 copy-start.15
  224.7 4.5 %copy-start.11 = (bf16[768,512]{1,0:T(8,128)(2,1)S(1)}, bf16[768,512]{1,0:T(8,128)(2,1)}, u32[]{:S(2)}) copy-start(bf16[768,512]{1,0:T(8,128)(2,1)} %copy.92) | copy-start | bytes 2359300
  224.7 4.9 %copy-start.8 = (bf16[512,576]{1,0:T(8,128)(2,1)S(1)}, bf16[512,576]{1,0:T(8,128)(2,1)}, u32[]{:S(2)}) copy-start(bf16[512,576]{1,0:T(8,128)(2,1)} %copy-done.7) | copy-start | bytes 1769476
  224.7 66.2 %all-to-all-start.1 = ((bf16[8,2,96,768]{3,2,1,0:T(8,128)(2,1)}), bf16[8,2,96,768]{3,2,1,0:T(8,128)(2,1)}, u32[]{:S(2)}, u32[]{:S(2)}) async-start(bf16[8,2,96,768]{3,2,1,0:T(8,128)(2,1)} %pad_maximum_fusion), calls=%async_computation.1 | async-start | bytes 4718592 | tf_op jit(solution)/shard_map/all_to_all | solution.py:596
  268.9 21.1 %copy-start.14 = (f32[128,768]{1,0:T(8,128)S(1)}, f32[128,768]{1,0:T(8,128)}, u32[]{:S(2)}) copy-start(f32[128,768]{1,0:T(8,128)} %get-tuple-element.117) | copy-start | bytes 1179652

commit v2 on v1

--- a/solution.py
+++ b/solution.py
@@ -61,11 +61,12 @@
     return (me < size - 1).astype(jnp.int32) + (me > 0).astype(jnp.int32)
 
 
-def line_gather(axis, size, x_ref, out_ref, send_sem, recv_sem):
+def line_gather(axis, size, items):
     me = lax.axis_index(axis)
-    rows = x_ref.shape[0] // pieces
-
-    def hop(way, step, piece):
+    rows = items[0][0].shape[0] // pieces
+
+    def hop(item, way, step, piece):
+        x_ref, out_ref, send_sem, recv_sem = item
         side = 1 - 2 * way
         block = me - side * step
         part = pl.ds(piece * rows, rows)
@@ -78,7 +79,8 @@
             device_id_type=pl.DeviceIdType.MESH,
         )
 
-    def arrival(way, step, piece):
+    def arrival(item, way, step, piece):
+        x_ref, out_ref, send_sem, recv_sem = item
         side = 1 - 2 * way
         block = me - side * (step + 1)
         part = pl.ds(piece * rows, rows)
@@ -102,27 +104,29 @@
         return me + step + 1 <= size - 1
 
     for step in range(size):
-        for piece in range(pieces):
-            for way in range(2):
-                if step > 0:
-
-                    @pl.when(receives(way, step - 1))
-                    def landed(way=way, step=step, piece=piece):
-                        arrival(way, step - 1, piece).wait_recv()
-
-                if step < size - 1:
+        for item in items:
+            for piece in range(pieces):
+                for way in range(2):
+                    if step > 0:
+
+                        @pl.when(receives(way, step - 1))
+                        def landed(item=item, way=way, step=step, piece=piece):
+                            arrival(item, way, step - 1, piece).wait_recv()
+
+                    if step < size - 1:
+
+                        @pl.when(sends(way, step))
+                        def forward(item=item, way=way, step=step, piece=piece):
+                            hop(item, way, step, piece).start()
+
+    for step in range(size - 1):
+        for item in items:
+            for piece in range(pieces):
+                for way in range(2):
 
                     @pl.when(sends(way, step))
-                    def forward(way=way, step=step, piece=piece):
-                        hop(way, step, piece).start()
-
-    for step in range(size - 1):
-        for piece in range(pieces):
-            for way in range(2):
-
-                @pl.when(sends(way, step))
-                def gone(way=way, step=step, piece=piece):
-                    hop(way, step, piece).wait_send()
+                    def gone(item=item, way=way, step=step, piece=piece):
+                        hop(item, way, step, piece).wait_send()
 
 
 def greet_direct(barrier, axis, size):
@@ -377,11 +381,13 @@
         )
         own.start()
         copies.append(own)
-    for num, (axis, kind) in enumerate(plan):
-        if kind == "line":
-            line_gather(
-                axis, size_of[axis], ins[num], outs[num], line_send.at[num], line_recv.at[num]
-            )
+    lines = [num for num, (unused, kind) in enumerate(plan) if kind == "line"]
+    if lines:
+        line_gather(
+            plan[lines[0]][0],
+            size_of[plan[lines[0]][0]],
+            [(ins[num], outs[num], line_send.at[num], line_recv.at[num]) for num in lines],
+        )
     for copy in copies:
         copy.wait()
 
@@ -585,35 +591,18 @@
         grad_rows.reshape(group_count, share_pad, model_width),
         "dp",
     )
+    inner_grad = dot_tn(rows_mine, grad_pre).astype(bf)
+    outer_grad = dot_tn(grad_mine, inner_act).astype(bf)
     grads_returned = dot_tn(
         place, back_grads.reshape(group_count * share_pad, model_width)
     ).astype(bf)
-    (slots_local,) = line_sum(
-        11, grads_returned.reshape(tensor_count, local_rows, model_width), "tensor"
-    )
-    inner_grad = dot_tn(rows_mine, grad_pre).astype(bf)
-    outer_grad = dot_tn(grad_mine, inner_act).astype(bf)
-    weight_back = lax.all_to_all(
-        jnp.stack(
-            [
-                inner_grad.reshape(group_count, width_share, hidden_share),
-                outer_grad.reshape(group_count, width_share, hidden_share),
-            ],
-            axis=1,
-        ),
+    slots_local, inner_back = line_sum(
+        11,
+        grads_returned.reshape(tensor_count, local_rows, model_width),
+        "tensor",
+        inner_grad.reshape(group_count, width_share, hidden_share),
         "dp",
-        split_axis=0,
-        concat_axis=0,
-        tiled=True,
-    )
-    weight_sum = jnp.sum(
-        weight_back.reshape(
-            expert_count, serve_count, 2, width_share, hidden_share
-        ).astype(jnp.float32),
-        axis=1,
-    )
-    inner_sum = weight_sum[:, 0]
-    outer_sum = weight_sum[:, 1].transpose(0, 2, 1)
+    )
     gate_local = lax.dynamic_slice_in_dim(gate_value, my_start, local_rows, 0)
     layer_out = (middle + gate_local[:, None] * expert_local).astype(bf)
     cot_local = cotangent.astype(jnp.float32)
@@ -632,7 +621,16 @@
     grad_two_local = slots_local + router_term
     grad_mid, grad_gain_two = norm_backward(grad_two_local, middle, scale_two, gain_expert)
     grad_middle = cot_local + grad_mid
-    (grad_mid_full,) = exchange(7, [(grad_middle.astype(bf), "tensor", "line")])
+    grad_mid_full, outer_back = exchange(
+        7,
+        [
+            (grad_middle.astype(bf), "tensor", "line"),
+            (outer_grad.reshape(group_count, width_share, hidden_share), "dp", "swap"),
+        ],
+    )
+    paired = (expert_count, serve_count, width_share, hidden_share)
+    inner_sum = jnp.sum(inner_back.reshape(paired).astype(jnp.float32), axis=1)
+    outer_sum = jnp.sum(outer_back.reshape(paired).astype(jnp.float32), axis=1).transpose(0, 2, 1)
     grad_mid_full = grad_mid_full.reshape(group_rows, model_width)
     grad_out_w = dot_tn(grad_mid_full, mixed_all)
     grad_qkv, grad_one_sent, diagonals = pl.pallas_call(

time: 296 us -> 294 us (level)
  starting transfers between devices: 9 us -> 4.5 us
  local copies, waits for them, and re-layouts: 16.3 us -> 20.1 us
    pallas_call x4, Pallas kernels: 98 us -> 81.1 us  [line_sum(): pl.pallas_call(functools.partial(line_sum_kernel, axis, size, beside), ou...]
    pallas_call x7, Pallas kernels: 117 us -> 132 us  [exchange(): pl.pallas_call(functools.partial(exchange_kernel, plan, sizes), out_shape...]
    unnamed x62 -> x98, local copies, waits for them, and re-layouts: 3.3 us -> 8.05 us
    all_to_all x1 -> x0, starting transfers between devices: 4.5 us -> none  [body(): lax.all_to_all(jnp.stack([inner_grad.reshape(group_count, width_share, hi...]
  transfers between devices with their start and end apart: 2 -> 1, of which waited for: 0 -> 0; matrix products, arithmetic and copies ran while one was open for 8% -> 4% of each run, Pallas kernels for 37% -> 19%
where the time goes in v2:
time: 294 us
  Pallas kernels  225 us (77%)
  matrix products  25.8 us (9%)
  local copies, waits for them, and re-layouts  20.1 us (7%)
  other arithmetic  17 us (6%)
  starting transfers between devices  4.5 us (2%)
    pallas_call x7, Pallas kernels, exchange(): pl.pallas_call(functools.partial(exchange_kernel, plan, sizes), out_shape...  132 us
    pallas_call x4, Pallas kernels, line_sum(): pl.pallas_call(functools.partial(line_sum_kernel, axis, size, beside), ou...  81.1 us
    dot_general x6, matrix products, dot_tn(): lax.dot_general(left, right, (((0,), (0,)), ((), ())), preferred_element_...  9.86 us
    unnamed x98, local copies, waits for them, and re-layouts  8.05 us
    dot_general x6, matrix products, dot_nn(): return jnp.dot(left, right, preferred_element_type=jnp.float32)  7.94 us
    pallas_call x1, Pallas kernels, body(): pl.pallas_call(functools.partial(attend_back_kernel, head_width), out_sha...  6.01 us
  transfers between devices with their start and end apart: 1, of which 0 were waited for; matrix products, arithmetic and copies ran while one was open for 4% of the time, Pallas kernels for 19%

profile of v2, /device:TPU:0, one launch (start us, length us, event | category | flops | bytes accessed | tf_op | source)
XLA Modules:
  0.0 293.8 jit_solution(14460313496342495192)
XLA Ops:
  4.0 1.4 pad_maximum_fusion
  7.2 36.0 %shard_map.247 = (bf16[4,128,768]{2,1,0:T(8,128)(2,1)}, bf16[8,96,896]{2,1,0:T(8,128)(2,1)}, bf16[4,128,768]{2,1,0:T(8,128)(2,1)}) custom-call(bf16[128,768]{1,0:T(8,128)(2,1)} %fusion.17.refs_0_, bf16[96,896]{1,0:T(8,128)(2,1)} %concatenate.11.refs_1_, bf16[128,768]{1,0:T(8,128)(2,1)} %refs_2_.1), custom_call_target="tpu_custom_call" | custom-call | tf_op jit(solution)/shard_map/pallas_call | solution.py:407
  43.2 1.6 broadcast_in_dim.25
  44.9 4.5 %all-to-all-start = ((bf16[8,2,96,768]{3,2,1,0:T(8,128)(2,1)}), bf16[8,2,96,768]{3,2,1,0:T(8,128)(2,1)}, u32[]{:S(2)}, u32[]{:S(2)}) async-start(bf16[8,2,96,768]{3,2,1,0:T(8,128)(2,1)} %bitcast.103), calls=%async_computation | async-start | bytes 4718592 | tf_op jit(solution)/shard_map/all_to_all | solution.py:511
  49.4 1.9 fusion.37
  51.6 5.5 %shard_map.248 = (bf16[512,576]{1,0:T(8,128)(2,1)S(1)}, f32[3,512,512]{2,1,0:T(8,128)}, bf16[512,192]{1,0:T(8,128)(2,1)S(1)}, bf16[512,768]{1,0:T(8,128)(2,1)S(1)}) custom-call(bf16[512,768]{1,0:T(8,128)(2,1)S(1)} %bitcast.90, bf16[768,896]{1,0:T(8,128)(2,1)S(1)} %bitcast.86, f32[3,8,1024]{2,1,0:T(8,128)S(1)} %copy.71.base_ref, s32[512,1]{1,0:T(8,128)S(1)} %copy.72.doc_col, ...), custom_call_target="tpu_custom_call" | custom-call | tf_op jit(solution)/shard_map/pallas_call | solution.py:520
  57.8 17.4 %shard_map.249 = f32[128,768]{1,0:T(8,128)S(1)} custom-call(bf16[4,128,768]{2,1,0:T(8,128)(2,1)S(1)} %bitcast.97), custom_call_target="tpu_custom_call" | custom-call | tf_op jit(solution)/shard_map/pallas_call | solution.py:262
  77.0 1.6 convolution_convert_fusion.5
  78.7 19.2 %shard_map.250 = (bf16[4,128,768]{2,1,0:T(8,128)(2,1)}, bf16[8,80,768]{2,1,0:T(8,128)(2,1)}) custom-call(bf16[128,768]{1,0:T(8,128)(2,1)} %multiply_convert_fusion.2.refs_0_, bf16[8,80,768]{2,1,0:T(8,128)(2,1)} %bitcast.115), custom_call_target="tpu_custom_call" | custom-call | tf_op jit(solution)/shard_map/pallas_call | solution.py:407
  97.9 1.5 fusion.42
  101.8 1.6 convolution_convert_fusion.4
  103.4 15.1 %shard_map.251 = (bf16[8,80,768]{2,1,0:T(8,128)(2,1)}, f32[8,1,80]{2,1,0:T(1,128)}) custom-call(bf16[8,80,768]{2,1,0:T(8,128)(2,1)} %bitcast.114, f32[8,1,80]{2,1,0:T(1,128)} %reshape.196.refs_1_), custom_call_target="tpu_custom_call" | custom-call | tf_op jit(solution)/shard_map/pallas_call | solution.py:407
  118.6 1.9 multiply_convert_fusion
  120.5 1.9 fusion.41
  123.6 1.9 fusion.6
  125.5 2.3 convolution_convert_fusion.3
  127.8 2.3 convolution_convert_fusion
  131.0 2.1 convolution_convert_fusion.1
  133.2 15.5 %shard_map.252 = bf16[8,80,768]{2,1,0:T(8,128)(2,1)} custom-call(bf16[8,80,768]{2,1,0:T(8,128)(2,1)} %bitcast.113), custom_call_target="tpu_custom_call" | custom-call | tf_op jit(solution)/shard_map/pallas_call | solution.py:407
  148.8 2.1 convolution_convert_fusion.8
  150.9 20.4 %shard_map.253 = (f32[128,768]{1,0:T(8,128)S(1)}, bf16[8,80,768]{2,1,0:T(8,128)(2,1)S(1)}) custom-call(bf16[4,128,768]{2,1,0:T(8,128)(2,1)S(1)} %bitcast.96, bf16[8,80,768]{2,1,0:T(8,128)(2,1)S(1)} %bitcast.95), custom_call_target="tpu_custom_call" | custom-call | tf_op jit(solution)/shard_map/pallas_call | solution.py:262
  173.2 2.2 convolution_convert_fusion.7
  176.7 24.2 %shard_map.254 = (f32[128,768]{1,0:T(8,128)S(1)}, bf16[8,96,768]{2,1,0:T(8,128)(2,1)S(1)}) custom-call(bf16[4,128,768]{2,1,0:T(8,128)(2,1)S(1)} %bitcast.99, bf16[8,96,768]{2,1,0:T(8,128)(2,1)S(1)} %bitcast.94), custom_call_target="tpu_custom_call" | custom-call | tf_op jit(solution)/shard_map/pallas_call | solution.py:262
  200.9 1.7 multiply_reduce_fusion
  203.6 27.0 %shard_map.255 = (bf16[4,128,768]{2,1,0:T(8,128)(2,1)}, bf16[8,96,768]{2,1,0:T(8,128)(2,1)}) custom-call(bf16[128,768]{1,0:T(8,128)(2,1)} %get-tuple-element.112.refs_0_, bf16[8,96,768]{2,1,0:T(8,128)(2,1)} %bitcast.106), custom_call_target="tpu_custom_call" | custom-call | tf_op jit(solution)/shard_map/pallas_call | solution.py:407
  230.6 2.4 copy.75
  234.1 6.0 %shard_map.256 = (bf16[512,576]{1,0:T(8,128)(2,1)S(1)}, bf16[512,768]{1,0:T(8,128)(2,1)S(1)}, f32[3,8,1024]{2,1,0:T(8,128)S(1)}) custom-call(bf16[512,768]{1,0:T(8,128)(2,1)S(1)} %bitcast.93, bf16[768,896]{1,0:T(8,128)(2,1)S(1)} %bitcast.89, bf16[512,576]{1,0:T(8,128)(2,1)S(1)} %copy-done.6, f32[3,512,512]{2,1,0:T(8,128)} %get-tuple-element.51.prob_ref), custom_call_target="tpu_custom_call" | custom-call | tf_op jit(solution)/shard_map/pallas_call | solution.py:636
  242.0 19.2 %shard_map.257 = (f32[128,768]{1,0:T(8,128)S(1)}, bf16[8,96,768]{2,1,0:T(8,128)(2,1)S(1)}) custom-call(bf16[4,128,768]{2,1,0:T(8,128)(2,1)S(1)} %bitcast.98, bf16[8,96,768]{2,1,0:T(8,128)(2,1)S(1)} %pad_maximum_fusion.1.refs_1_), custom_call_target="tpu_custom_call" | custom-call | tf_op jit(solution)/shard_map/pallas_call | solution.py:262
  263.3 12.6 %shard_map.258 = f32[4,40,128]{2,1,0:T(8,128)} custom-call(f32[40,128]{1,0:T(8,128)} %fusion.30.refs_0_), custom_call_target="tpu_custom_call" | custom-call | tf_op jit(solution)/shard_map/pallas_call | solution.py:407
  275.9 1.5 reduce_sum.156.refs_0_
  277.4 7.0 %shard_map.259 = f32[8,40,128]{2,1,0:T(8,128)} custom-call(f32[40,128]{1,0:T(8,128)} %reduce_sum.156.refs_0_), custom_call_target="tpu_custom_call" | custom-call | tf_op jit(solution)/shard_map/pallas_call | solution.py:407
  288.4 2.6 convert_reduce_fusion
  (147 shorter events, 28.2 us)
Async XLA Ops:
  0.6 48.7 %copy-start = (f32[32,12]{0,1:T(8,128)S(1)}, f32[32,12]{0,1:T(8,128)}, u32[]{:S(2)}) copy-start(f32[32,12]{0,1:T(8,128)} %param.26) | copy-start | bytes 4612
  2.3 3.2 %copy-start.34 = (f32[128]{0:T(128)}, f32[128]{0:T(128)S(1)}, u32[]{:S(2)}) copy-start(f32[128]{0:T(128)S(1)} %get-tuple-element.128) | copy-start | bytes 1540
  44.8 6.6 %copy-start.9 = (s32[512]{0:T(512)S(1)}, s32[512]{0:T(512)}, u32[]{:S(2)}) copy-start(s32[512]{0:T(512)} %param.17) | copy-start | bytes 6148
  44.8 6.7 %copy-start.2 = (bf16[4,128,768]{2,1,0:T(8,128)(2,1)S(1)}, bf16[4,128,768]{2,1,0:T(8,128)(2,1)}, u32[]{:S(2)}) copy-start(bf16[4,128,768]{2,1,0:T(8,128)(2,1)} %get-tuple-element.37) | copy-start | bytes 2359300
  44.9 75.6 %all-to-all-start = ((bf16[8,2,96,768]{3,2,1,0:T(8,128)(2,1)}), bf16[8,2,96,768]{3,2,1,0:T(8,128)(2,1)}, u32[]{:S(2)}, u32[]{:S(2)}) async-start(bf16[8,2,96,768]{3,2,1,0:T(8,128)(2,1)} %bitcast.103), calls=%async_computation | async-start | bytes 4718592 | tf_op jit(solution)/shard_map/all_to_all | solution.py:511
  51.6 23.8 %copy-start.24 = (bf16[512,512]{1,0:T(8,128)(2,1)S(1)}, bf16[512,512]{1,0:T(8,128)(2,1)}, u32[]{:S(2)}) copy-start(bf16[512,512]{1,0:T(8,128)(2,1)} %constant.81.clone) | copy-start | bytes 1572868
  51.6 23.8 %copy-start.31 = (s32[512,1]{0,1:T(1,128)S(1)}, s32[512,1]{0,1:T(1,128)}, u32[]{:S(2)}) copy-start(s32[512,1]{0,1:T(1,128)} %param.18) | copy-start | bytes 6148
  57.8 20.8 %copy-start.5 = (bf16[512,576]{1,0:T(8,128)(2,1)}, bf16[512,576]{1,0:T(8,128)(2,1)S(1)}, u32[]{:S(2)}) copy-start(bf16[512,576]{1,0:T(8,128)(2,1)S(1)} %get-tuple-element.50.proj_ref) | copy-start | bytes 1769476
  57.8 18.4 %copy-start.29 = (f32[768]{0:T(1024)S(1)}, f32[768]{0:T(1024)}, u32[]{:S(2)}) copy-start(f32[768]{0:T(1024)} %param.25) | copy-start | bytes 9220
  57.8 19.2 %copy-start.46 = (bf16[4,128,768]{2,1,0:T(8,128)(2,1)S(1)}, bf16[4,128,768]{2,1,0:T(8,128)(2,1)}, u32[]{:S(2)}) copy-start(bf16[4,128,768]{2,1,0:T(8,128)(2,1)} %get-tuple-element.40) | copy-start | bytes 2359300
  75.4 3.3 %copy-start.11 = (f32[128,768]{1,0:T(8,128)}, f32[128,768]{1,0:T(8,128)S(1)}, u32[]{:S(2)}) copy-start(f32[128,768]{1,0:T(8,128)S(1)} %get-tuple-element.117) | copy-start | bytes 1179652
  76.2 21.7 %copy-start.39 = (f32[128]{0:T(128)}, f32[128]{0:T(128)S(1)}, u32[]{:S(2)}) copy-start(f32[128]{0:T(128)S(1)} %get-tuple-element.130) | copy-start | bytes 1540
  97.9 3.9 %copy-start.23 = (bf16[4,128,768]{2,1,0:T(8,128)(2,1)S(1)}, bf16[4,128,768]{2,1,0:T(8,128)(2,1)}, u32[]{:S(2)}) copy-start(bf16[4,128,768]{2,1,0:T(8,128)(2,1)} %get-tuple-element.41) | copy-start | bytes 2359300
  99.5 72.9 %copy-start.32 = (f32[512,4]{0,1:T(4,128)}, f32[512,4]{0,1:T(4,128)S(1)}, u32[]{:S(2)}) copy-start(f32[512,4]{0,1:T(4,128)S(1)} %get-tuple-element.115) | copy-start | bytes 24580
  100.6 71.8 %copy-start.37 = (f32[128]{0:T(128)}, f32[128]{0:T(128)S(1)}, u32[]{:S(2)}) copy-start(f32[128]{0:T(128)S(1)} %dynamic_slice.16) | copy-start | bytes 1540
  101.8 16.8 %copy-start.20 = (bf16[8,80,768]{2,1,0:T(8,128)(2,1)S(1)}, bf16[8,80,768]{2,1,0:T(8,128)(2,1)}, u32[]{:S(2)}) copy-start(bf16[8,80,768]{2,1,0:T(8,128)(2,1)} %get-tuple-element.45) | copy-start | bytes 2949124
  118.6 53.8 %copy-start.36 = (pred[512,4]{0,1:T(4,128)(4,1)}, pred[512,4]{0,1:T(4,128)(4,1)S(1)}, u32[]{:S(2)}) copy-start(pred[512,4]{0,1:T(4,128)(4,1)S(1)} %iota_compare_fusion.6) | copy-start | bytes 6148
  148.7 23.5 %copy-start.16 = (bf16[128,768]{1,0:T(8,128)(2,1)S(1)}, bf16[128,768]{1,0:T(8,128)(2,1)}, u32[]{:S(2)}) copy-start(bf16[128,768]{1,0:T(8,128)(2,1)} %refs_2_.1) | copy-start | bytes 589828
  148.8 23.7 %copy-start.18 = (bf16[128,768]{1,0:T(8,128)(2,1)S(1)}, bf16[128,768]{1,0:T(8,128)(2,1)}, u32[]{:S(2)}) copy-start(bf16[128,768]{1,0:T(8,128)(2,1)} %multiply_convert_fusion.2.refs_0_) | copy-start | bytes 589828
  173.2 27.6 %copy-start.12 = (f32[128,768]{1,0:T(8,128)S(1)}, f32[128,768]{1,0:T(8,128)}, u32[]{:S(2)}) copy-start(f32[128,768]{1,0:T(8,128)} %copy-done.11) | copy-start | bytes 1179652
  173.2 27.6 %copy-start.38 = (f32[128]{0:T(128)S(1)}, f32[128]{0:T(128)}, u32[]{:S(2)}) copy-start(f32[128]{0:T(128)} %copy-done.37) | copy-start | bytes 1540
  173.2 27.7 %copy-start.40 = (f32[128]{0:T(128)S(1)}, f32[128]{0:T(128)}, u32[]{:S(2)}) copy-start(f32[128]{0:T(128)} %copy-done.39) | copy-start | bytes 1540
  173.2 29.3 %copy-start.17 = (bf16[128,768]{1,0:T(8,128)(2,1)S(1)}, bf16[128,768]{1,0:T(8,128)(2,1)}, u32[]{:S(2)}) copy-start(bf16[128,768]{1,0:T(8,128)(2,1)} %refs_2_.1) | copy-start | bytes 589828
  175.4 27.2 %copy-start.44 = (f32[128]{0:T(128)S(1)}, f32[128]{0:T(128)}, u32[]{:S(2)}) copy-start(f32[128]{0:T(128)} %get-tuple-element.129) | copy-start | bytes 1540
  176.7 24.2 %copy-start.42 = (f32[128]{0:T(128)S(1)}, f32[128]{0:T(128)}, u32[]{:S(2)}) copy-start(f32[128]{0:T(128)} %copy-done.41) | copy-start | bytes 1540
  234.1 6.0 %copy-start.22 = (bf16[768,512]{1,0:T(8,128)(2,1)S(1)}, bf16[768,512]{1,0:T(8,128)(2,1)}, u32[]{:S(2)}) copy-start(bf16[768,512]{1,0:T(8,128)(2,1)} %copy.73) | copy-start | bytes 2359300
  241.7 19.5 %copy-start.35 = (f32[128]{0:T(128)S(1)}, f32[128]{0:T(128)}, u32[]{:S(2)}) copy-start(f32[128]{0:T(128)} %copy-done.34) | copy-start | bytes 1540
  241.7 19.6 %copy-start.14 = (f32[32,8,1024]{2,0,1:T(8,128)S(1)}, f32[32,8,1024]{2,0,1:T(8,128)}, u32[]{:S(2)}) copy-start(f32[32,8,1024]{2,0,1:T(8,128)} %constant.80.clone) | copy-start | bytes 3145732
  242.0 20.7 %copy-start.28 = (f32[3072]{0:T(1024)S(1)}, f32[3072]{0:T(1024)}, u32[]{:S(2)}) copy-start(f32[3072]{0:T(1024)} %reshape.210) | copy-start | bytes 36868
  242.0 20.7 %copy-start.33 = (f32[768]{0:T(1024)S(1)}, f32[768]{0:T(1024)}, u32[]{:S(2)}) copy-start(f32[768]{0:T(1024)} %get-tuple-element.108) | copy-start | bytes 9220
  288.4 4.5 %copy-start.19 = (f32[128,768]{1,0:T(8,128)S(1)}, f32[128,768]{1,0:T(8,128)}, u32[]{:S(2)}) copy-start(f32[128,768]{1,0:T(8,128)} %get-tuple-element.113) | copy-start | bytes 1179652
  288.4 4.5 %copy-start.43 = (f32[128]{0:T(128)S(1)}, f32[128]{0:T(128)}, u32[]{:S(2)}) copy-start(f32[128]{0:T(128)} %get-tuple-element.127) | copy-start | bytes 1540
  (16 other events, 22.9 us)
